TPU v7x, 256 devices: a whole 4x4x8 slice. The times are simulated.
256 devices in a mesh: dp: 32 (over y, z), tensor: 8 (over x, core).
Axes of the slice: x: 4, y: 4, z: 8, core: 2. Of those that a mesh axis runs over, the one named last changes fastest.
Arguments:
- tree_ids: int32 [32, 64], P('dp'), may hold values from 0 to 65535, as said below
- ancestors: int32 [32, 64, 64], P('dp'), may hold values from 0 to 1, as said below
- lengths: int32 [32], P('dp'), may hold values from 64 to 1024, as said below
- table: bfloat16 [65536, 4096], P('dp', 'tensor'), may hold values from -3 to 3
- gain: bfloat16 [4096], replicated, may hold values from 0.25 to 1.75
- w_query: bfloat16 [4096, 4096], P(None, 'tensor'), may hold values from -0.09375 to 0.09375
- w_kv: bfloat16 [2, 4096, 1024], P(None, None, 'tensor'), may hold values from -0.09375 to 0.09375
- w_out: bfloat16 [4096, 4096], P('tensor'), may hold values from -0.09375 to 0.09375
- key_cache: bfloat16 [32, 8, 1024, 128], P('dp', 'tensor'), may hold values from -480 to 480
- value_cache: bfloat16 [32, 8, 1024, 128], P('dp', 'tensor'), may hold values from -6 to 6
Outputs:
- layer_output: bfloat16 [2048, 4096], P('dp', 'tensor')
Inputs may be any that keep to these rules, and one draw needn't show every extreme that they name: `tree_ids`: split the vocabulary into equal consecutive parts, one for each index of dp; of the nodes of the rows of one index of dp, at most 4 have ids in any one part, and exactly 4 in some part. Row n of each row's matrix marks node n and all its ancestors in that row's tree; node 0 is the root and every other node's parent has a smaller index. `lengths`: some row has all 1024 slots live.
All inputs are finite; a program needn't handle non-finite values.
Results may differ from a plain program's by a relative error of at most 0.004.
The roundings to bfloat16 on the way count: a program that leaves them out, or rounds other values in their place, can miss the bound.
Values may be sent and summed in bfloat16 or wider, within the bound.
No kernel may reach another device: no remote copies, remote signals or barrier semaphores. Data moves between devices by JAX's collectives and lax.ppermute only.
A program may use at most 64 MiB of HBM per device.

v0:
```python
import math

import jax
import jax.numpy as jnp
from jax import lax
from jax.sharding import PartitionSpec as P

D = 4096


EPS = 1e-05
NEG = -1e30
THETA = 500000.0


def rotary(values, positions):
    half_dim = values.shape[-1] // 2
    freq_index = jnp.arange(half_dim, dtype=jnp.float32)
    inverse = jnp.exp(freq_index * (-2.0 * math.log(THETA) / values.shape[-1]))
    angles = positions[:, None] * inverse[None, :]
    cosine = jnp.cos(angles)[:, None, :]
    sine_part = jnp.sin(angles)[:, None, :]
    lower_half = values[..., :half_dim]
    upper_half = values[..., half_dim:]
    return jnp.concatenate(
        [
            lower_half * cosine - upper_half * sine_part,
            upper_half * cosine + lower_half * sine_part,
        ],
        axis=-1,
    )


def contract(left_side, right_side):
    return lax.dot_general(
        left_side, right_side, (((1,), (1,)), ((), ())), preferred_element_type=jnp.float32
    )


def to_groups(tensor_in, kv_heads, head_dim):
    row_count, node_count, width_all = tensor_in.shape
    per_group = width_all // (kv_heads * head_dim)
    grouped = tensor_in.reshape(row_count, node_count, kv_heads, per_group, head_dim).transpose(
        0, 2, 3, 1, 4
    )
    return grouped.reshape(row_count, kv_heads, per_group * node_count, head_dim)


def from_groups(tensor_in, node_count):
    row_count, kv_heads, group_rows, head_dim = tensor_in.shape
    grouped = tensor_in.reshape(row_count, kv_heads, group_rows // node_count, node_count, head_dim)
    return grouped.transpose(0, 3, 1, 2, 4).reshape(row_count, node_count, -1)


def attend(query_group, keys_tree, values_tree, keys_cache, values_cache, live_len, tree_mask):
    score_scale = keys_cache.shape[-1] ** (-0.5)
    slot_count = keys_cache.shape[0]
    cache_scores = contract(query_group, keys_cache) * score_scale
    columns = jnp.arange(slot_count, dtype=jnp.int32)
    cache_scores = jnp.where(columns[None, :] < live_len, cache_scores, NEG)
    tree_scores = contract(query_group, keys_tree) * score_scale
    groups = query_group.shape[0] // tree_mask.shape[0]
    tree_scores = jnp.where(jnp.tile(tree_mask, (groups, 1)) > 0, tree_scores, NEG)
    row_top = jnp.maximum(jnp.max(cache_scores, axis=1), jnp.max(tree_scores, axis=1))[:, None]
    cache_exp = jnp.exp(cache_scores - row_top)
    tree_exp = jnp.exp(tree_scores - row_top)
    denominator = jnp.sum(cache_exp, axis=1) + jnp.sum(tree_exp, axis=1)
    cache_weights = cache_exp.astype(jnp.bfloat16)
    weighted = jnp.dot(
        tree_exp.astype(jnp.bfloat16), values_tree, preferred_element_type=jnp.float32
    )
    weighted = weighted + jnp.dot(cache_weights, values_cache, preferred_element_type=jnp.float32)
    return (weighted / denominator[:, None]).astype(jnp.bfloat16)


def shards(tree_ids, ancestors, lengths, table, gain, w_query, w_kv, w_out, key_cache, value_cache):
    row_count, node_count = tree_ids.shape
    token_count = row_count * node_count
    head_dim = key_cache.shape[3]
    kv_local = key_cache.shape[1]
    all_ids = lax.all_gather(tree_ids, "dp", axis=0, tiled=True).reshape(-1)
    vocab_rows = table.shape[0]
    my_index = lax.axis_index("dp")
    offsets = all_ids - my_index * vocab_rows
    owned = (offsets >= 0) & (offsets < vocab_rows)
    picked = jnp.take(table, jnp.clip(offsets, 0, vocab_rows - 1), axis=0)
    partial_value = jnp.where(owned[:, None], picked, jnp.zeros_like(picked))
    emb_share = lax.psum_scatter(
        partial_value.astype(jnp.float32).astype(jnp.bfloat16),
        "dp",
        scatter_dimension=0,
        tiled=True,
    )
    gain_full = gain.astype(jnp.float32)
    features = lax.all_gather(emb_share, "tensor", axis=1, tiled=True).astype(jnp.float32)
    inv_rms = lax.rsqrt(jnp.sum(features * features, axis=1) / D + EPS)
    normed = (features * inv_rms[:, None] * gain_full[None, :]).astype(jnp.bfloat16)
    queries = jnp.dot(normed, w_query, preferred_element_type=jnp.float32)
    keys_new = jnp.dot(normed, w_kv[0], preferred_element_type=jnp.float32)
    values_raw = jnp.dot(normed, w_kv[1], preferred_element_type=jnp.float32)
    values_new = values_raw.astype(jnp.bfloat16).reshape(row_count, node_count, -1)
    node_depth = jnp.sum(ancestors, axis=2) - 1
    positions = (lengths[:, None] + node_depth).reshape(-1).astype(jnp.float32)
    query_heads = w_query.shape[1] // head_dim
    queries = rotary(queries.reshape(token_count, query_heads, head_dim), positions).astype(
        jnp.bfloat16
    )
    queries = queries.reshape(row_count, node_count, query_heads * head_dim)
    keys_new = rotary(keys_new.reshape(token_count, kv_local, head_dim), positions).astype(
        jnp.bfloat16
    )
    keys_new = keys_new.reshape(row_count, node_count, kv_local * head_dim)
    query_groups = to_groups(queries, kv_local, head_dim)
    key_groups = to_groups(keys_new, kv_local, head_dim)
    value_groups = to_groups(values_new, kv_local, head_dim)

    def per_row(row_items):
        row_q, row_k, row_v, row_kc, row_vc, live_len, tree_mask = row_items

        def per_head(head_items):
            return attend(
                head_items[0],
                head_items[1],
                head_items[2],
                head_items[3],
                head_items[4],
                live_len,
                tree_mask,
            )

        return lax.map(per_head, (row_q, row_k, row_v, row_kc, row_vc))

    contexts = lax.map(
        per_row,
        (query_groups, key_groups, value_groups, key_cache, value_cache, lengths, ancestors),
    )
    contexts = from_groups(contexts, node_count).reshape(token_count, query_heads * head_dim)
    partial_out = jnp.dot(contexts, w_out, preferred_element_type=jnp.float32)
    attention = lax.psum_scatter(partial_out, "tensor", scatter_dimension=1, tiled=True)
    return (emb_share.astype(jnp.float32) + attention).astype(jnp.bfloat16)


def solution(mesh):
    in_specs = (
        P("dp", None),
        P("dp", None, None),
        P("dp"),
        P("dp", "tensor"),
        P(),
        P(None, "tensor"),
        P(None, None, "tensor"),
        P("tensor", None),
        P("dp", "tensor", None, None),
        P("dp", "tensor", None, None),
    )
    out_specs = P("dp", "tensor")
    return jax.shard_map(shards, mesh=mesh, in_specs=in_specs, out_specs=out_specs, check_vma=False)
```

profile of v0, /device:TPU:1, one launch (start us, length us, event | category | flops | bytes accessed | tf_op | source)
XLA Modules:
  0.0 343.2 jit_solution(14227830214254407760)
XLA Ops:
  6.5 0.0 copy-start
  6.5 0.0 reduce-scatter.3.cloned.1.call-start
  6.5 34.1 %all-gather = s32[32,1,64]{2,1,0:T(1,128)S(1)} all-gather(s32[1,1,64]{2,1,0:T(1,128)} %bitcast.56), channel_id=1, replica_groups=mesh['dp'=32,'tensor'=8] {'dp'}, dimensions={0}, use_global_device_ids=true | all-gather | bytes 8448 | tf_op jit(solution)/shard_map/all_gather | solution.py:81
  40.6 0.1 and_reduce_fusion
  40.7 0.5 broadcast.243
  41.2 0.7 fusion.48
  41.9 0.1 min.18
  42.0 0.1 min.16
  42.1 0.1 and.19
  42.2 0.0 copy-done
  42.2 9.2 %gather_fusion = bf16[2048,512]{1,0:T(8,128)(2,1)} fusion(bf16[2048,512]{1,0:T(8,128)(2,1)S(1)} %copy-done, s32[2048]{0:T(1024)S(1)} %broadcast_clamp_fusion), kind=kCustom, calls=%fused_computation | custom fusion | bytes 4202496 | tf_op jit(solution)/shard_map/jit(_take)/gather | solution.py:86
  51.3 3.0 select_select_fusion
  54.3 0.0 copy-start.6
  54.3 0.0 copy-start.5
  54.3 0.0 reduce-scatter.3.cloned.1.call-update
  54.3 0.0 reduce-scatter.5.cloned.1.call-start
  54.4 0.6 copy-done.6
  55.7 0.0 copy-done.5
  55.7 0.1 reduce_sum.41
  55.8 0.1 copy.16
  55.9 0.1 gt.14
  56.1 0.2 multiply_cosine_fusion.1
  56.3 215.6 %reduce-scatter.3.cloned.1.call-done = bf16[64,512]{1,0:T(8,128)(2,1)} async-done(((bf16[2048,512]{1,0:T(8,128)(2,1)}), bf16[64,512]{1,0:T(8,128)(2,1)}) %reduce-scatter.3.cloned.1.call-update) | async-done | bytes 65552 | tf_op jit(solution)/shard_map/reduce_scatter | solution.py:88
  271.9 19.2 %all_gather.7 = bf16[64,4096]{1,0:T(8,128)(2,1)S(1)} all-gather(bf16[64,512]{1,0:T(8,128)(2,1)} %reduce-scatter.3.cloned.1.call-done), channel_id=1, replica_groups=mesh['dp'=32,'tensor'=8] {'tensor'}, dimensions={1}, use_global_device_ids=true | all-gather | bytes 589824 | tf_op jit(solution)/shard_map/all_gather | solution.py:95
  291.1 0.0 copy-start.1
  291.1 0.2 fusion.5
  291.4 3.1 fusion.46
  294.4 0.0 copy-start.3
  294.5 0.1 fusion.49
  294.6 0.0 copy-done.1
  294.7 1.6 convolution_bitcast_fusion
  296.2 0.2 fusion.41
  296.5 0.1 pad_maximum_fusion
  296.6 0.0 copy-done.3
  296.6 0.4 fusion.50
  297.0 0.0 copy-start.4
  297.0 0.2 fusion.51
  297.2 2.6 fusion.4
  299.8 0.3 fusion.14
  300.1 0.0 copy-done.4
  300.1 1.3 fusion.2
  301.4 0.1 copy.19
  301.5 0.0 copy-start.2
  301.5 4.1 %fusion.22 = f32[64,4096]{1,0:T(8,128)} fusion(bf16[512,4096]{1,0:T(8,128)(2,1)} %param.17, bf16[8,8,4,128]{3,2,1,0:T(4,128)(2,1)S(1)} %bitcast.53), kind=kOutput, calls=%fused_computation.32 | convolution fusion | flops 268435456 | bytes 5308416 | tf_op jit(solution)/shard_map/dot_general | solution.py:138
  305.5 0.0 reduce-scatter.5.cloned.1.call-update
  305.6 29.2 %reduce-scatter.5.cloned.1.call-done = f32[64,512]{1,0:T(8,128)} async-done(((f32[64,4096]{1,0:T(8,128)}), f32[64,512]{1,0:T(8,128)}) %reduce-scatter.5.cloned.1.call-update) | async-done | bytes 131088 | tf_op jit(solution)/shard_map/reduce_scatter | solution.py:139
  334.8 0.0 copy-done.2
  334.8 1.5 add_convert_fusion
  (15 shorter events, 0.2 us)
Async XLA Ops:
  6.5 35.6 %copy-start = (bf16[2048,512]{1,0:T(8,128)(2,1)S(1)}, bf16[2048,512]{1,0:T(8,128)(2,1)}, u32[]{:S(2)}) copy-start(bf16[2048,512]{1,0:T(8,128)(2,1)} %param.13) | copy-start | bytes 6291460
  6.5 265.4 %reduce-scatter.3.cloned.1.call-start = ((), (), s32[]{:S(2)}) async-start(), calls=%async_computation.2 | async-start | bytes 2162688 | tf_op jit(solution)/shard_map/reduce_scatter | solution.py:88
  54.3 0.7 copy-start.6
  54.3 1.4 copy-start.5
  54.3 280.4 %reduce-scatter.5.cloned.1.call-start = ((), (), s32[]{:S(2)}) async-start(), calls=%async_computation.3 | async-start | bytes 1179648 | tf_op jit(solution)/shard_map/reduce_scatter | solution.py:139
  291.1 3.5 %copy-start.1 = (bf16[64,4096]{1,0:T(8,128)(2,1)}, bf16[64,4096]{1,0:T(8,128)(2,1)S(1)}, u32[]{:S(2)}) copy-start(bf16[64,4096]{1,0:T(8,128)(2,1)S(1)} %all_gather.7) | copy-start | bytes 1572868
  294.4 2.1 copy-start.3
  297.0 3.2 copy-start.4
  301.5 33.3 %copy-start.2 = (bf16[64,512]{1,0:T(8,128)(2,1)S(1)}, bf16[64,512]{1,0:T(8,128)(2,1)}, u32[]{:S(2)}) copy-start(bf16[64,512]{1,0:T(8,128)(2,1)} %reduce-scatter.3.cloned.1.call-done) | copy-start | bytes 196612
Sparse Core Ops, SparseCore 0:
  54.4 217.4 reduce-scatter.2
  305.7 29.0 reduce-scatter.4
where the time goes:
time: 345 us; the launch traced here: 343 us
  waiting for transfers between devices  245 us (71%)
  blocking collectives  53.3 us (15%)
  between operations  14.3 us (4%)
  matrix products  13.1 us (4%)
  local copies, waits for them, and re-layouts  11 us (3%)
  other arithmetic  6.54 us (2%)
    reduce_scatter x1, waiting for transfers between devices, shards(): lax.psum_scatter(partial_value.astype(jnp.float32).astype(jnp.bfloat16),...  216 us
    all_gather x1, blocking collectives, shards(): all_ids = lax.all_gather(tree_ids, 'dp', axis=0, tiled=True).reshape(-1)  34.1 us
    reduce_scatter x1, waiting for transfers between devices, shards(): lax.psum_scatter(partial_out, 'tensor', scatter_dimension=1, tiled=True)  29.2 us
    all_gather x1, blocking collectives, shards(): lax.all_gather(emb_share, 'tensor', axis=1, tiled=True).astype(jnp.float32)  19.2 us
    gather x1, local copies, waits for them, and re-layouts, shards(): picked = jnp.take(table, jnp.clip(offsets, 0, vocab_rows - 1), axis=0)  9.16 us
  transfers between devices with their start and end apart: 2, of which 2 were waited for; matrix products, arithmetic and copies ran while one was open for 0% of the time, Pallas kernels for 0%

commit v1 on v0

v1 whole, which is shorter than its diff:
```python
import functools
import math

import jax
import jax.numpy as jnp
from jax import lax
from jax.experimental import pallas as pl
from jax.experimental.pallas import tpu as pltpu
from jax.sharding import PartitionSpec as P

D = 4096
HD = 128
CAP = 4
EPS = 1e-05
NEG = -1e30
THETA = 500000.0
BF = jnp.bfloat16
F32 = jnp.float32


def iota(shape, dim):
    return lax.broadcasted_iota(jnp.int32, shape, dim)


def rows_kernel(idx_ref, ids_ref, table_ref, out_ref):
    vocab = table_ref.shape[0]
    n_dst, nodes = ids_ref.shape
    off = ids_ref[...] - idx_ref[0] * vocab
    owned = (off >= 0) & (off < vocab)
    before = jnp.where(iota((nodes, nodes), 0) < iota((nodes, nodes), 1), 1.0, 0.0).astype(BF)
    rank = jnp.dot(jnp.where(owned, 1.0, 0.0).astype(BF), before, preferred_element_type=F32)
    high = jnp.where(owned, rank * (vocab // 256) + (off >> 8).astype(F32), -1.0).astype(BF)
    low = jnp.where(owned, (off & 255).astype(F32), 0.0).astype(BF)
    n_out = n_dst * 2 * CAP
    spread = jnp.where(
        (iota((n_out, n_dst), 0) >> 3) == iota((n_out, n_dst), 1), 1.0, 0.0
    ).astype(BF)
    code = 256.0 * jnp.dot(spread, high, preferred_element_type=F32) + jnp.dot(
        spread, low, preferred_element_type=F32
    )
    code = code.astype(jnp.int32)
    slot = (iota((n_out, nodes), 0) & (CAP - 1)) * vocab
    rel = code - slot
    entry = jnp.max(
        jnp.where((rel >= 0) & (rel < vocab), rel, -1).astype(F32), axis=1, keepdims=True
    ).astype(jnp.int32)
    pick = jnp.where(iota((n_out, vocab), 1) == entry, 1.0, 0.0).astype(BF)
    rows = jnp.dot(pick, table_ref[...], preferred_element_type=F32)
    half = rows.shape[1] // 2
    upper = (iota((n_out, half), 0) & CAP) > 0
    out_ref[...] = jnp.where(upper, rows[:, half:], rows[:, :half]).astype(BF)


def pick_kernel(ids_ref, recv_ref, out_ref, *, vocab):
    nodes = ids_ref.shape[1]
    n_in, half = recv_ref.shape
    ids_row = jnp.broadcast_to(ids_ref[...], (nodes, nodes)) // vocab
    owner_row = ids_row.astype(F32)
    owner_col = owner_row.T
    same = (owner_row == owner_col) & (iota((nodes, nodes), 1) < iota((nodes, nodes), 0))
    rank = jnp.sum(jnp.where(same, 1.0, 0.0), axis=1, keepdims=True)
    slot = (owner_col[:, 0:1] * 8.0 + rank).astype(jnp.int32)
    columns = iota((nodes, n_in), 1)
    recv = recv_ref[...]
    low = jnp.where(columns == slot, 1.0, 0.0).astype(BF)
    high = jnp.where(columns == slot + CAP, 1.0, 0.0).astype(BF)
    out_ref[:, :half] = jnp.dot(low, recv, preferred_element_type=F32).astype(BF)
    out_ref[:, half:] = jnp.dot(high, recv, preferred_element_type=F32).astype(BF)


def rotate(x, cos, sin):
    return x * cos + pltpu.roll(x, HD // 2, 1) * sin


def layer_kernel(
    idx_ref, len_ref, mine_ref, other_ref, gain_ref, wq_ref, wkv_ref, wout_ref, kc_ref, vc_ref,
    anc_ref, cos_ref, sin_ref, ctx_ref, send_ref, normed,
):
    me = idx_ref[0]
    n_x, nodes, width = mine_ref.shape
    total = jnp.zeros((nodes, 1), F32)
    for j in range(n_x):
        for ref in (mine_ref, other_ref):
            piece = ref[j].astype(F32)
            total = total + jnp.sum(piece * piece, axis=1, keepdims=True)
    inv_rms = lax.rsqrt(total / D + EPS)
    for j in range(n_x):
        for c, ref in enumerate((mine_ref, other_ref)):
            owner = (me ^ (2 * j)) ^ c
            cols = pl.ds(pl.multiple_of(owner * width, width), width)
            gain = gain_ref[:, cols].astype(F32)
            normed[:, cols] = (ref[j].astype(F32) * inv_rms * gain).astype(BF)
    x = normed[...]
    queries = jnp.dot(x, wq_ref[...], preferred_element_type=F32)
    keys = jnp.dot(x, wkv_ref[0], preferred_element_type=F32)
    values = jnp.dot(x, wkv_ref[1], preferred_element_type=F32).astype(BF)
    cos = cos_ref[...]
    sin = sin_ref[...]
    heads = queries.shape[1] // HD
    keys = rotate(keys, cos, sin).astype(BF)
    group = jnp.concatenate(
        [rotate(queries[:, h * HD : (h + 1) * HD], cos, sin).astype(BF) for h in range(heads)], axis=0
    )
    contract = (((1,), (1,)), ((), ()))
    scale = HD ** (-0.5)
    slots = kc_ref.shape[0]
    s_cache = lax.dot_general(group, kc_ref[...], contract, preferred_element_type=F32) * scale
    s_cache = jnp.where(iota((1, slots), 1) < len_ref[0], s_cache, NEG)
    s_tree = lax.dot_general(group, keys, contract, preferred_element_type=F32) * scale
    mask = jnp.concatenate([anc_ref[...]] * heads, axis=0)
    s_tree = jnp.where(mask > 0, s_tree, NEG)
    top = jnp.maximum(
        jnp.max(s_cache, axis=1, keepdims=True), jnp.max(s_tree, axis=1, keepdims=True)
    )
    e_cache = jnp.exp(s_cache - top)
    e_tree = jnp.exp(s_tree - top)
    denominator = jnp.sum(e_cache, axis=1, keepdims=True) + jnp.sum(e_tree, axis=1, keepdims=True)
    weighted = jnp.dot(e_cache.astype(BF), vc_ref[...], preferred_element_type=F32)
    weighted = weighted + jnp.dot(e_tree.astype(BF), values, preferred_element_type=F32)
    ctx = (weighted / denominator).astype(BF)
    ctx = jnp.concatenate([ctx[h * nodes : (h + 1) * nodes] for h in range(heads)], axis=1)
    ctx_ref[...] = ctx
    for j in range(n_x):
        cols = pl.ds(pl.multiple_of(((me ^ (2 * j)) ^ 1) * width, width), width)
        send_ref[j] = jnp.dot(ctx, wout_ref[:, cols], preferred_element_type=F32).astype(BF)


def out_kernel(idx_ref, ctx_ref, wout_ref, out_ref):
    out_ref[0] = jnp.dot(ctx_ref[...], wout_ref[...], preferred_element_type=F32)


def swap(n, k):
    return [(i, i ^ k) for i in range(n)]


def shards(tree_ids, ancestors, lengths, table, gain, w_query, w_kv, w_out, key_cache, value_cache):
    n_dp = lax.axis_size("dp")
    n_tp = lax.axis_size("tensor")
    n_x = n_tp // 2
    nodes = tree_ids.shape[1]
    vocab, width = table.shape
    me = lax.axis_index("tensor")
    me_arr = me.astype(jnp.int32).reshape(1)
    part = lax.axis_index("dp").astype(jnp.int32).reshape(1)
    vmem = pl.BlockSpec(memory_space=pltpu.VMEM)
    smem = pl.BlockSpec(memory_space=pltpu.SMEM)

    all_ids = lax.all_gather(tree_ids, "dp", axis=0, tiled=True)
    rows = pl.pallas_call(
        rows_kernel,
        out_shape=jax.ShapeDtypeStruct((n_dp * 2 * CAP, width // 2), BF),
        in_specs=[smem, vmem, vmem],
        out_specs=vmem,
        name="rows",
    )(part, all_ids, table)
    recv = lax.all_to_all(
        rows.reshape(n_dp, 2 * CAP, width // 2), "dp", split_axis=0, concat_axis=0, tiled=True
    )
    emb = pl.pallas_call(
        functools.partial(pick_kernel, vocab=vocab),
        out_shape=jax.ShapeDtypeStruct((nodes, width), BF),
        in_specs=[vmem, vmem],
        out_specs=vmem,
        name="pick",
    )(tree_ids, recv.reshape(n_dp * 2 * CAP, width // 2))

    mine = jnp.stack(
        [emb] + [lax.ppermute(emb, "tensor", swap(n_tp, 2 * j)) for j in range(1, n_x)], 0
    )
    other = lax.ppermute(mine, "tensor", swap(n_tp, 1))

    depth = jnp.sum(ancestors[0], axis=1) - 1
    positions = (lengths[0] + depth).astype(F32)
    freq_index = jnp.arange(HD // 2, dtype=F32)
    inverse = jnp.exp(freq_index * (-2.0 * math.log(THETA) / HD))
    angles = positions[:, None] * inverse[None, :]
    cosine = jnp.cos(angles)
    sine = jnp.sin(angles)
    cos = jnp.concatenate([cosine, cosine], axis=1)
    sin = jnp.concatenate([-sine, sine], axis=1)

    ctx, send = pl.pallas_call(
        layer_kernel,
        out_shape=(
            jax.ShapeDtypeStruct((nodes, width), BF),
            jax.ShapeDtypeStruct((n_x, nodes, width), BF),
        ),
        in_specs=[smem, smem] + [vmem] * 11,
        out_specs=(vmem, vmem),
        scratch_shapes=[pltpu.VMEM((nodes, n_tp * width), BF)],
        compiler_params=pltpu.CompilerParams(vmem_limit_bytes=40 * 1024 * 1024),
        name="layer",
    )(
        me_arr, lengths, mine, other, gain.reshape(1, -1), w_query, w_kv, w_out,
        key_cache[0, 0], value_cache[0, 0], ancestors[0], cos, sin,
    )
    came = lax.ppermute(send, "tensor", swap(n_tp, 1))
    own = pl.pallas_call(
        out_kernel,
        grid_spec=pltpu.PrefetchScalarGridSpec(
            num_scalar_prefetch=1,
            grid=(n_x,),
            in_specs=[
                pl.BlockSpec((nodes, width), lambda j, m: (0, 0)),
                pl.BlockSpec((width, width), lambda j, m: (0, m[0] ^ (2 * j))),
            ],
            out_specs=pl.BlockSpec((1, nodes, width), lambda j, m: (j, 0, 0)),
        ),
        out_shape=jax.ShapeDtypeStruct((n_x, nodes, width), F32),
        cost_estimate=pl.CostEstimate(
            flops=2 * nodes * width * width * n_x, bytes_accessed=2 * width * width * n_x, transcendentals=0
        ),
        name="project",
    )(me_arr, ctx, w_out)
    pair = own + came.astype(F32)
    attention = pair[0]
    for j in range(1, n_x):
        attention = attention + lax.ppermute(
            pair[j].astype(BF), "tensor", swap(n_tp, 2 * j)
        ).astype(F32)
    return (emb.astype(F32) + attention).astype(BF)


def solution(mesh):
    in_specs = (
        P("dp", None),
        P("dp", None, None),
        P("dp"),
        P("dp", "tensor"),
        P(),
        P(None, "tensor"),
        P(None, None, "tensor"),
        P("tensor", None),
        P("dp", "tensor", None, None),
        P("dp", "tensor", None, None),
    )
    out_specs = P("dp", "tensor")
    return jax.shard_map(shards, mesh=mesh, in_specs=in_specs, out_specs=out_specs, check_vma=False)
```

time: 345 us -> 104 us (0.30)
  waiting for transfers between devices: 245 us -> 15.5 us
  starting transfers between devices: 0.04 us -> 26.3 us
  blocking collectives: 53.3 us -> 36 us
  between operations: 14.3 us -> 0.74 us
  matrix products: 13.1 us -> 0 us
  Pallas kernels: 0 us -> 11.6 us
    reduce_scatter x2 -> x0, waiting for transfers between devices: 245 us -> none  [the longest x1 216 us: shards(): lax.psum_scatter(partial_value.astype(jnp.float32).astype(jnp.bfloat16),...]
    ppermute x0 -> x8, starting transfers between devices: none -> 19.5 us  [the longest x1 12.6 us: shards(): other = lax.ppermute(mine, 'tensor', swap(n_tp, 1))]
    all_gather x2 -> x1, blocking collectives: 53.3 us -> 36 us  [shards(): all_ids = lax.all_gather(tree_ids, 'dp', axis=0, tiled=True)]
    dot_general x7 -> x0, matrix products: 13.1 us -> none  [the longest x1 4.06 us: shards(): partial_out = jnp.dot(contexts, w_out, preferred_element_type=jnp.float32)]
    pallas_call x0 -> x4, Pallas kernels: none -> 11.6 us  [the longest x1 3.82 us: shards(): pl.pallas_call(out_kernel, grid_spec=pltpu.PrefetchScalarGridSpec(num_sca...]
    gather x1 -> x0, local copies, waits for them, and re-layouts: 9.16 us -> none  [shards(): picked = jnp.take(table, jnp.clip(offsets, 0, vocab_rows - 1), axis=0)]
    ppermute x0 -> x8, waiting for transfers between devices: none -> 8.61 us  [the longest x3 4.34 us: shards(): lax.ppermute(emb, 'tensor', swap(n_tp, 2 * j))]
    unnamed x14 -> x18, local copies, waits for them, and re-layouts: 0.65 us -> 8.3 us
  transfers between devices with their start and end apart: 2 -> 9, of which waited for: 2 -> 7; matrix products, arithmetic and copies ran while one was open for 0% -> 2% of each run, Pallas kernels for 0% -> 4%
where the time goes in v1:
time: 104 us; the launch traced here: 103 us
  blocking collectives  36 us (35%)
  starting transfers between devices  26.3 us (25%)
  waiting for transfers between devices  15.5 us (15%)
  Pallas kernels  11.6 us (11%)
  local copies, waits for them, and re-layouts  9.02 us (9%)
  other arithmetic  3.83 us (4%)
    all_gather x1, blocking collectives, shards(): all_ids = lax.all_gather(tree_ids, 'dp', axis=0, tiled=True)  36 us
    ppermute x1, starting transfers between devices, shards(): other = lax.ppermute(mine, 'tensor', swap(n_tp, 1))  12.6 us
    unnamed x18, local copies, waits for them, and re-layouts  8.3 us
    all_to_all x1, waiting for transfers between devices, shards(): lax.all_to_all(rows.reshape(n_dp, 2 * CAP, width // 2), 'dp', split_axis=...  6.91 us
    all_to_all x1, starting transfers between devices, shards(): lax.all_to_all(rows.reshape(n_dp, 2 * CAP, width // 2), 'dp', split_axis=...  6.73 us
    ppermute x3, waiting for transfers between devices, shards(): lax.ppermute(emb, 'tensor', swap(n_tp, 2 * j))  4.34 us
    pallas_call x1, Pallas kernels, shards(): pl.pallas_call(out_kernel, grid_spec=pltpu.PrefetchScalarGridSpec(num_sca...  3.82 us
    ppermute x3, waiting for transfers between devices, shards(): lax.ppermute(pair[j].astype(BF), 'tensor', swap(n_tp, 2 * j)).astype(F32)  3.39 us
  transfers between devices with their start and end apart: 9, of which 7 were waited for; matrix products, arithmetic and copies ran while one was open for 2% of the time, Pallas kernels for 4%

profile of v1, /device:TPU:1, one launch (start us, length us, event | category | flops | bytes accessed | tf_op | source)
XLA Modules:
  0.0 102.9 jit_solution(2737704259239651214)
XLA Ops:
  0.0 0.0 copy-start.2
  0.0 36.0 %all-gather = s32[32,1,64]{2,1,0:T(1,128)} all-gather(s32[1,1,64]{2,1,0:T(1,128)} %bitcast.43), channel_id=1, replica_groups=mesh['dp'=32,'tensor'=8] {'dp'}, dimensions={0}, use_global_device_ids=true | all-gather | bytes 8448 | tf_op jit(solution)/shard_map/all_gather | solution.py:148
  36.0 3.3 %rows.1 = bf16[256,256]{1,0:T(8,128)(2,1)} custom-call(s32[1]{0:T(128)} %bitcast.idx_ref, s32[32,64]{1,0:T(8,128)} %bitcast.39, bf16[2048,512]{1,0:T(8,128)(2,1)} %table_ref.1), custom_call_target="tpu_custom_call" | custom-call | tf_op jit(solution)/shard_map/rows/pallas_call | solution.py:149
  39.3 6.7 %all-to-all-start = ((bf16[32,8,256]{2,1,0:T(8,128)(2,1)}), bf16[32,8,256]{2,1,0:T(8,128)(2,1)S(1)}, u32[]{:S(2)}, u32[]{:S(2)}) async-start(bf16[32,8,256]{2,1,0:T(8,128)(2,1)} %bitcast.37), calls=%async_computation | async-start | bytes 262144 | tf_op jit(solution)/shard_map/all_to_all | solution.py:156
  46.6 0.7 reshape.32.gain_ref
  47.4 0.9 reduce_sum.9
  48.2 6.9 %all-to-all-done = bf16[32,8,256]{2,1,0:T(8,128)(2,1)S(1)} async-done(((bf16[32,8,256]{2,1,0:T(8,128)(2,1)}), bf16[32,8,256]{2,1,0:T(8,128)(2,1)S(1)}, u32[]{:S(2)}, u32[]{:S(2)}) %all-to-all-start) | async-done | bytes 131104 | tf_op jit(solution)/shard_map/all_to_all | solution.py:156
  55.1 0.0 copy-start.8
  55.1 0.6 copy-done.8
  55.8 1.9 %pick.1 = bf16[64,512]{1,0:T(8,128)(2,1)} custom-call(s32[1,64]{1,0:T(1,128)} %ids_ref.1, bf16[256,256]{1,0:T(8,128)(2,1)} %bitcast.38), custom_call_target="tpu_custom_call" | custom-call | tf_op jit(solution)/shard_map/pick/pallas_call | solution.py:159
  57.7 2.5 %collective-permute-start.2 = (bf16[64,512]{1,0:T(8,128)(2,1)}, bf16[64,512]{1,0:T(8,128)(2,1)S(1)}, u32[]{:S(2)}, u32[]{:S(2)}) collective-permute-start(bf16[64,512]{1,0:T(8,128)(2,1)} %pick.1), channel_id=1, source_target_pairs={{0,6},{1,7},{2,4},{3,5},{4,2},{5,3},{6,0},{7,1},{8,14},{9,15},{10,... | collective-permute-start | bytes 196616 | tf_op jit(solution)/shard_map/ppermute | solution.py:168
  60.2 0.5 collective-permute-start.1
  60.7 0.3 collective-permute-start
  61.0 1.6 %collective-permute-done.2 = bf16[64,512]{1,0:T(8,128)(2,1)S(1)} collective-permute-done((bf16[64,512]{1,0:T(8,128)(2,1)}, bf16[64,512]{1,0:T(8,128)(2,1)S(1)}, u32[]{:S(2)}, u32[]{:S(2)}) %collective-permute-start.2) | collective-permute-done | bytes 65568 | tf_op jit(solution)/shard_map/ppermute | solution.py:168
  62.5 2.8 %collective-permute-done.1 = bf16[64,512]{1,0:T(8,128)(2,1)S(1)} collective-permute-done((bf16[64,512]{1,0:T(8,128)(2,1)}, bf16[64,512]{1,0:T(8,128)(2,1)S(1)}, u32[]{:S(2)}, u32[]{:S(2)}) %collective-permute-start.1) | collective-permute-done | bytes 65568 | tf_op jit(solution)/shard_map/ppermute | solution.py:168
  65.3 0.0 collective-permute-done
  65.3 0.9 pad_maximum_fusion.mine_ref
  66.2 12.6 %collective-permute-start.3 = (bf16[4,64,512]{2,1,0:T(8,128)(2,1)S(1)}, bf16[4,64,512]{2,1,0:T(8,128)(2,1)S(1)}, u32[]{:S(2)}, u32[]{:S(2)}) collective-permute-start(bf16[4,64,512]{2,1,0:T(8,128)(2,1)S(1)} %pad_maximum_fusion.mine_ref), channel_id=1, source_target_pairs={{0,1},{1,0},{2,3},{3,2},{4,5},{5,4},{6,7},{7,6},{8,9},{9,8},{10,11... | collective-permute-start | bytes 786440 | tf_op jit(solution)/shard_map/ppermute | solution.py:170
  78.8 0.2 fusion.5
  79.0 0.1 pad_maximum_fusion.1
  79.1 0.9 collective-permute-done.3.other_ref
  79.9 0.0 copy-done.2
  79.9 0.0 copy-start
  79.9 2.2 %copy-done = bf16[512,4096]{1,0:T(8,128)(2,1)S(1)} copy-done((bf16[512,4096]{1,0:T(8,128)(2,1)S(1)}, bf16[512,4096]{1,0:T(8,128)(2,1)}, u32[]{:S(2)}) %copy-start) | copy-done | bytes 4194328
  82.1 0.0 copy-start.1
  82.1 2.2 %copy-done.1 = bf16[4096,512]{1,0:T(8,128)(2,1)S(1)} copy-done((bf16[4096,512]{1,0:T(8,128)(2,1)S(1)}, bf16[4096,512]{1,0:T(8,128)(2,1)}, u32[]{:S(2)}) %copy-start.1) | copy-done | bytes 4194328
  84.3 0.0 copy-start.3
  84.3 0.9 copy-done.3
  85.3 0.0 copy-start.4
  85.3 0.9 copy-done.4
  86.2 0.0 copy-start.5
  86.2 0.8 copy-done.5
  87.0 2.5 %layer.1 = (bf16[64,512]{1,0:T(8,128)(2,1)S(1)}, bf16[4,64,512]{2,1,0:T(8,128)(2,1)S(1)}) custom-call(s32[1]{0:T(128)} %bitcast.5.idx_ref, s32[1]{0:T(128)} %copy.12.len_ref, bf16[4,64,512]{2,1,0:T(8,128)(2,1)S(1)} %pad_maximum_fusion.mine_ref, bf16[4,64,512]{2,1,0:T(8,128)(2,1)S(1)} %collective-permute-done.3.other_ref, ...), custom_call_target="tpu_custom_call" | custom-call | tf_op jit(solution)/shard_map/layer/pallas_call | solution.py:182
  89.5 0.0 copy-start.6
  89.5 0.6 copy-done.6
  90.1 0.0 copy-start.7
  90.1 0.4 collective-permute-start.4
  90.5 3.8 %project.1 = f32[4,64,512]{2,1,0:T(8,128)} custom-call(s32[1]{0:T(128)} %bitcast.5.idx_ref, bf16[64,512]{1,0:T(8,128)(2,1)} %copy-done.6, bf16[512,4096]{1,0:T(8,128)(2,1)} %wout_ref.3), custom_call_target="tpu_custom_call" | custom-call | flops 134217728 | bytes 2097152 | tf_op jit(solution)/shard_map/project/pallas_call | solution.py:198
  94.3 0.0 collective-permute-done.4
  94.4 1.1 %fusion.6 = (bf16[4,64,512]{2,1,0:T(8,128)(2,1)S(1)}, f32[4,64,512]{2,1,0:T(8,128)S(1)}) fusion(f32[4,64,512]{2,1,0:T(8,128)} %project.1, bf16[4,64,512]{2,1,0:T(8,128)(2,1)S(1)} %collective-permute-done.4), kind=kLoop, calls=%fused_computation.18 | loop fusion | flops 393216 | bytes 1572864 | tf_op jit(solution)/shard_map/convert.2
  95.5 0.1 collective-permute-start.5
  95.6 2.0 %collective-permute-start.7 = (bf16[64,512]{1,0:T(8,128)(2,1)S(1)}, bf16[64,512]{1,0:T(8,128)(2,1)S(1)}, u32[]{:S(2)}, u32[]{:S(2)}) collective-permute-start(bf16[64,512]{1,0:T(8,128)(2,1)S(1)} %get-tuple-element.12), channel_id=1, source_target_pairs={{0,6},{1,7},{2,4},{3,5},{4,2},{5,3},{6,0},{7,1},{8,14},{9,15},{10,... | collective-permute-start | bytes 196616 | tf_op jit(solution)/shard_map/ppermute | solution.py:218
  97.6 1.2 %collective-permute-start.6 = (bf16[64,512]{1,0:T(8,128)(2,1)S(1)}, bf16[64,512]{1,0:T(8,128)(2,1)S(1)}, u32[]{:S(2)}, u32[]{:S(2)}) collective-permute-start(bf16[64,512]{1,0:T(8,128)(2,1)S(1)} %get-tuple-element.13), channel_id=1, source_target_pairs={{0,4},{1,5},{2,6},{3,7},{4,0},{5,1},{6,2},{7,3},{8,12},{9,13},{10,... | collective-permute-start | bytes 196616 | tf_op jit(solution)/shard_map/ppermute | solution.py:218
  98.9 0.3 collective-permute-done.5
  99.2 0.9 collective-permute-done.7
  100.0 2.2 %collective-permute-done.6 = bf16[64,512]{1,0:T(8,128)(2,1)S(1)} collective-permute-done((bf16[64,512]{1,0:T(8,128)(2,1)S(1)}, bf16[64,512]{1,0:T(8,128)(2,1)S(1)}, u32[]{:S(2)}, u32[]{:S(2)}) %collective-permute-start.6) | collective-permute-done | bytes 65568 | tf_op jit(solution)/shard_map/ppermute | solution.py:218
  102.2 0.0 copy-done.7
  102.2 0.7 fusion.4
  (3 shorter events, 0.0 us)
Async XLA Ops:
  0.0 79.9 %copy-start.2 = (bf16[2,4096,128]{2,1,0:T(8,128)(2,1)S(1)}, bf16[2,4096,128]{2,1,0:T(8,128)(2,1)}, u32[]{:S(2)}) copy-start(bf16[2,4096,128]{2,1,0:T(8,128)(2,1)} %wkv_ref.1) | copy-start | bytes 6291460
  39.3 15.9 %all-to-all-start = ((bf16[32,8,256]{2,1,0:T(8,128)(2,1)}), bf16[32,8,256]{2,1,0:T(8,128)(2,1)S(1)}, u32[]{:S(2)}, u32[]{:S(2)}) async-start(bf16[32,8,256]{2,1,0:T(8,128)(2,1)} %bitcast.37), calls=%async_computation | async-start | bytes 262144 | tf_op jit(solution)/shard_map/all_to_all | solution.py:156
  55.1 0.6 copy-start.8
  57.7 4.8 %collective-permute-start.2 = (bf16[64,512]{1,0:T(8,128)(2,1)}, bf16[64,512]{1,0:T(8,128)(2,1)S(1)}, u32[]{:S(2)}, u32[]{:S(2)}) collective-permute-start(bf16[64,512]{1,0:T(8,128)(2,1)} %pick.1), channel_id=1, source_target_pairs={{0,6},{1,7},{2,4},{3,5},{4,2},{5,3},{6,0},{7,1},{8,14},{9,15},{10,... | collective-permute-start | bytes 196616 | tf_op jit(solution)/shard_map/ppermute | solution.py:168
  60.2 5.1 %collective-permute-start.1 = (bf16[64,512]{1,0:T(8,128)(2,1)}, bf16[64,512]{1,0:T(8,128)(2,1)S(1)}, u32[]{:S(2)}, u32[]{:S(2)}) collective-permute-start(bf16[64,512]{1,0:T(8,128)(2,1)} %pick.1), channel_id=1, source_target_pairs={{0,4},{1,5},{2,6},{3,7},{4,0},{5,1},{6,2},{7,3},{8,12},{9,13},{10,... | collective-permute-start | bytes 196616 | tf_op jit(solution)/shard_map/ppermute | solution.py:168
  60.7 4.6 %collective-permute-start = (bf16[64,512]{1,0:T(8,128)(2,1)}, bf16[64,512]{1,0:T(8,128)(2,1)S(1)}, u32[]{:S(2)}, u32[]{:S(2)}) collective-permute-start(bf16[64,512]{1,0:T(8,128)(2,1)} %pick.1), channel_id=1, source_target_pairs={{0,2},{1,3},{2,0},{3,1},{4,6},{5,7},{6,4},{7,5},{8,10},{9,11},{10,... | collective-permute-start | bytes 196616 | tf_op jit(solution)/shard_map/ppermute | solution.py:168
  66.2 13.7 %collective-permute-start.3 = (bf16[4,64,512]{2,1,0:T(8,128)(2,1)S(1)}, bf16[4,64,512]{2,1,0:T(8,128)(2,1)S(1)}, u32[]{:S(2)}, u32[]{:S(2)}) collective-permute-start(bf16[4,64,512]{2,1,0:T(8,128)(2,1)S(1)} %pad_maximum_fusion.mine_ref), channel_id=1, source_target_pairs={{0,1},{1,0},{2,3},{3,2},{4,5},{5,4},{6,7},{7,6},{8,9},{9,8},{10,11... | collective-permute-start | bytes 786440 | tf_op jit(solution)/shard_map/ppermute | solution.py:170
  79.9 2.2 %copy-start = (bf16[512,4096]{1,0:T(8,128)(2,1)S(1)}, bf16[512,4096]{1,0:T(8,128)(2,1)}, u32[]{:S(2)}) copy-start(bf16[512,4096]{1,0:T(8,128)(2,1)} %wout_ref.3) | copy-start | bytes 12582916
  82.1 2.2 %copy-start.1 = (bf16[4096,512]{1,0:T(8,128)(2,1)S(1)}, bf16[4096,512]{1,0:T(8,128)(2,1)}, u32[]{:S(2)}) copy-start(bf16[4096,512]{1,0:T(8,128)(2,1)} %wq_ref.1) | copy-start | bytes 12582916
  84.3 0.9 copy-start.3
  85.3 0.9 copy-start.4
  86.2 0.8 copy-start.5
  89.5 0.6 copy-start.6
  90.1 12.1 %copy-start.7 = (bf16[64,512]{1,0:T(8,128)(2,1)S(1)}, bf16[64,512]{1,0:T(8,128)(2,1)}, u32[]{:S(2)}) copy-start(bf16[64,512]{1,0:T(8,128)(2,1)} %pick.1) | copy-start | bytes 196612
  90.1 4.2 %collective-permute-start.4 = (bf16[4,64,512]{2,1,0:T(8,128)(2,1)S(1)}, bf16[4,64,512]{2,1,0:T(8,128)(2,1)S(1)}, u32[]{:S(2)}, u32[]{:S(2)}) collective-permute-start(bf16[4,64,512]{2,1,0:T(8,128)(2,1)S(1)} %get-tuple-element.8), channel_id=1, source_target_pairs={{0,1},{1,0},{2,3},{3,2},{4,5},{5,4},{6,7},{7,6},{8,9},{9,8},{10,11... | collective-permute-start | bytes 786440 | tf_op jit(solution)/shard_map/ppermute | solution.py:197
  95.5 3.6 %collective-permute-start.5 = (bf16[64,512]{1,0:T(8,128)(2,1)S(1)}, bf16[64,512]{1,0:T(8,128)(2,1)S(1)}, u32[]{:S(2)}, u32[]{:S(2)}) collective-permute-start(bf16[64,512]{1,0:T(8,128)(2,1)S(1)} %get-tuple-element.11), channel_id=1, source_target_pairs={{0,2},{1,3},{2,0},{3,1},{4,6},{5,7},{6,4},{7,5},{8,10},{9,11},{10,... | collective-permute-start | bytes 196616 | tf_op jit(solution)/shard_map/ppermute | solution.py:218
  95.6 4.4 %collective-permute-start.7 = (bf16[64,512]{1,0:T(8,128)(2,1)S(1)}, bf16[64,512]{1,0:T(8,128)(2,1)S(1)}, u32[]{:S(2)}, u32[]{:S(2)}) collective-permute-start(bf16[64,512]{1,0:T(8,128)(2,1)S(1)} %get-tuple-element.12), channel_id=1, source_target_pairs={{0,6},{1,7},{2,4},{3,5},{4,2},{5,3},{6,0},{7,1},{8,14},{9,15},{10,... | collective-permute-start | bytes 196616 | tf_op jit(solution)/shard_map/ppermute | solution.py:218
  97.6 4.6 %collective-permute-start.6 = (bf16[64,512]{1,0:T(8,128)(2,1)S(1)}, bf16[64,512]{1,0:T(8,128)(2,1)S(1)}, u32[]{:S(2)}, u32[]{:S(2)}) collective-permute-start(bf16[64,512]{1,0:T(8,128)(2,1)S(1)} %get-tuple-element.13), channel_id=1, source_target_pairs={{0,4},{1,5},{2,6},{3,7},{4,0},{5,1},{6,2},{7,3},{8,12},{9,13},{10,... | collective-permute-start | bytes 196616 | tf_op jit(solution)/shard_map/ppermute | solution.py:218

commit v2 on v1

--- a/solution.py
+++ b/solution.py
@@ -125,8 +125,59 @@
         send_ref[j] = jnp.dot(ctx, wout_ref[:, cols], preferred_element_type=F32).astype(BF)
 
 
+def load_kernel(count, *refs):
+    dst = refs[-1 - count : -1]
+    copies = [pltpu.make_async_copy(refs[i], dst[i], refs[-1].at[i]) for i in range(count)]
+    for copy in copies:
+        copy.start()
+    for copy in copies:
+        copy.wait()
+
+
+def load(arrays, after, mib):
+    return pl.pallas_call(
+        functools.partial(load_kernel, len(arrays)),
+        out_shape=tuple(jax.ShapeDtypeStruct(a.shape, a.dtype) for a in arrays),
+        in_specs=[pl.BlockSpec(memory_space=pltpu.HBM)] * len(arrays)
+        + [pl.BlockSpec(memory_space=pl.ANY)] * len(after),
+        out_specs=(pl.BlockSpec(memory_space=pltpu.VMEM),) * len(arrays),
+        scratch_shapes=[pltpu.SemaphoreType.DMA((len(arrays),))],
+        cost_estimate=pl.CostEstimate(
+            flops=0, bytes_accessed=sum(a.size * a.dtype.itemsize for a in arrays), transcendentals=0
+        ),
+        compiler_params=limit(mib),
+        name="load",
+    )(*arrays, *after)
+
+
 def out_kernel(idx_ref, ctx_ref, wout_ref, out_ref):
-    out_ref[0] = jnp.dot(ctx_ref[...], wout_ref[...], preferred_element_type=F32)
+    n_x, _, width = out_ref.shape
+    ctx = ctx_ref[...]
+    for j in range(n_x):
+        cols = pl.ds(pl.multiple_of((idx_ref[0] ^ (2 * j)) * width, width), width)
+        out_ref[j] = jnp.dot(ctx, wout_ref[:, cols], preferred_element_type=F32)
+
+
+def pair_kernel(own_ref, came_ref, *out_refs):
+    for j, ref in enumerate(out_refs):
+        ref[...] = (own_ref[j] + came_ref[j].astype(F32)).astype(ref.dtype)
+
+
+def stack_kernel(*refs):
+    out_ref = refs[-1]
+    for j in range(out_ref.shape[0]):
+        out_ref[j] = refs[j][...]
+
+
+def final_kernel(emb_ref, own_ref, *refs):
+    total = own_ref[...]
+    for ref in refs[:-1]:
+        total = total + ref[...].astype(F32)
+    refs[-1][...] = (emb_ref[...].astype(F32) + total).astype(BF)
+
+
+def limit(mib):
+    return pltpu.CompilerParams(vmem_limit_bytes=mib * 1024 * 1024)
 
 
 def swap(n, k):
@@ -145,14 +196,18 @@
     vmem = pl.BlockSpec(memory_space=pltpu.VMEM)
     smem = pl.BlockSpec(memory_space=pltpu.SMEM)
 
-    all_ids = lax.all_gather(tree_ids, "dp", axis=0, tiled=True)
+    all_ids = lax.all_to_all(
+        jnp.broadcast_to(tree_ids, (n_dp, nodes)), "dp", split_axis=0, concat_axis=0, tiled=True
+    )
+    (table_held,) = load((table,), (), 50)
     rows = pl.pallas_call(
         rows_kernel,
         out_shape=jax.ShapeDtypeStruct((n_dp * 2 * CAP, width // 2), BF),
         in_specs=[smem, vmem, vmem],
         out_specs=vmem,
+        compiler_params=limit(12),
         name="rows",
-    )(part, all_ids, table)
+    )(part, all_ids, table_held)
     recv = lax.all_to_all(
         rows.reshape(n_dp, 2 * CAP, width // 2), "dp", split_axis=0, concat_axis=0, tiled=True
     )
@@ -161,12 +216,19 @@
         out_shape=jax.ShapeDtypeStruct((nodes, width), BF),
         in_specs=[vmem, vmem],
         out_specs=vmem,
+        compiler_params=limit(4),
         name="pick",
     )(tree_ids, recv.reshape(n_dp * 2 * CAP, width // 2))
 
-    mine = jnp.stack(
-        [emb] + [lax.ppermute(emb, "tensor", swap(n_tp, 2 * j)) for j in range(1, n_x)], 0
-    )
+    w_query, w_kv, w_out = load((w_query, w_kv, w_out), (emb,), 41)
+    mine = pl.pallas_call(
+        stack_kernel,
+        in_specs=[vmem] * n_x + [pl.BlockSpec(memory_space=pl.ANY)],
+        out_specs=vmem,
+        out_shape=jax.ShapeDtypeStruct((n_x, nodes, width), BF),
+        compiler_params=limit(4),
+        name="stack",
+    )(emb, *[lax.ppermute(emb, "tensor", swap(n_tp, 2 * j)) for j in range(1, n_x)], w_kv)
     other = lax.ppermute(mine, "tensor", swap(n_tp, 1))
 
     depth = jnp.sum(ancestors[0], axis=1) - 1
@@ -188,7 +250,7 @@
         in_specs=[smem, smem] + [vmem] * 11,
         out_specs=(vmem, vmem),
         scratch_shapes=[pltpu.VMEM((nodes, n_tp * width), BF)],
-        compiler_params=pltpu.CompilerParams(vmem_limit_bytes=40 * 1024 * 1024),
+        compiler_params=limit(16),
         name="layer",
     )(
         me_arr, lengths, mine, other, gain.reshape(1, -1), w_query, w_kv, w_out,
@@ -197,28 +259,32 @@
     came = lax.ppermute(send, "tensor", swap(n_tp, 1))
     own = pl.pallas_call(
         out_kernel,
-        grid_spec=pltpu.PrefetchScalarGridSpec(
-            num_scalar_prefetch=1,
-            grid=(n_x,),
-            in_specs=[
-                pl.BlockSpec((nodes, width), lambda j, m: (0, 0)),
-                pl.BlockSpec((width, width), lambda j, m: (0, m[0] ^ (2 * j))),
-            ],
-            out_specs=pl.BlockSpec((1, nodes, width), lambda j, m: (j, 0, 0)),
-        ),
+        in_specs=[smem, vmem, vmem],
+        out_specs=vmem,
         out_shape=jax.ShapeDtypeStruct((n_x, nodes, width), F32),
         cost_estimate=pl.CostEstimate(
             flops=2 * nodes * width * width * n_x, bytes_accessed=2 * width * width * n_x, transcendentals=0
         ),
+        compiler_params=limit(8),
         name="project",
     )(me_arr, ctx, w_out)
-    pair = own + came.astype(F32)
-    attention = pair[0]
-    for j in range(1, n_x):
-        attention = attention + lax.ppermute(
-            pair[j].astype(BF), "tensor", swap(n_tp, 2 * j)
-        ).astype(F32)
-    return (emb.astype(F32) + attention).astype(BF)
+    pairs = pl.pallas_call(
+        pair_kernel,
+        in_specs=[vmem, vmem],
+        out_specs=(vmem,) * n_x,
+        out_shape=tuple(jax.ShapeDtypeStruct((nodes, width), F32 if j == 0 else BF) for j in range(n_x)),
+        compiler_params=limit(4),
+        name="pair",
+    )(own, came)
+    parts = [lax.ppermute(pairs[j], "tensor", swap(n_tp, 2 * j)) for j in range(1, n_x)]
+    return pl.pallas_call(
+        final_kernel,
+        in_specs=[vmem] * (n_x + 1),
+        out_specs=vmem,
+        out_shape=jax.ShapeDtypeStruct((nodes, width), BF),
+        compiler_params=limit(4),
+        name="final",
+    )(emb, pairs[0], *parts)
 
 
 def solution(mesh):

time: 104 us -> 64.4 us (0.62)
  blocking collectives: 36 us -> 0 us
  local copies, waits for them, and re-layouts: 9.02 us -> 2.96 us
  waiting for transfers between devices: 15.5 us -> 21.1 us
  other arithmetic: 3.83 us -> 0.4 us
  starting transfers between devices: 26.3 us -> 27.9 us
    all_gather x1 -> x0, blocking collectives: 36 us -> none  [shards(): all_ids = lax.all_gather(tree_ids, 'dp', axis=0, tiled=True)]
    all_to_all x0 -> x1, starting transfers between devices: none -> 12 us  [shards(): lax.all_to_all(jnp.broadcast_to(tree_ids, (n_dp, nodes)), 'dp', split_axi...]
    ppermute x1, starting transfers between devices: 12.6 us -> 4.26 us  [shards(): other = lax.ppermute(mine, 'tensor', swap(n_tp, 1))]
    all_to_all x0 -> x1, waiting for transfers between devices: none -> 6.95 us  [shards(): lax.all_to_all(jnp.broadcast_to(tree_ids, (n_dp, nodes)), 'dp', split_axi...]
    unnamed x18 -> x12, local copies, waits for them, and re-layouts: 8.3 us -> 1.61 us
    ppermute x3, waiting for transfers between devices: 4.34 us -> 0.01 us  [shards(): lax.ppermute(emb, 'tensor', swap(n_tp, 2 * j))]
    all_to_all x1, starting transfers between devices: 6.73 us -> 3.85 us  [shards(): lax.all_to_all(rows.reshape(n_dp, 2 * CAP, width // 2), 'dp', split_axis=...]
    pallas_call x1 -> x6, Pallas kernels: 3.82 us -> 6.4 us  [the longest x2 5.17 us: load(): pl.pallas_call(functools.partial(load_kernel, len(arrays)), out_shape=tup...]
  transfers between devices with their start and end apart: 9 -> 10, of which waited for: 7 -> 6; matrix products, arithmetic and copies ran while one was open for 2% -> 1% of each run, Pallas kernels for 4% -> 9%
where the time goes in v2:
time: 64.4 us; the launch traced here: 64.1 us
  starting transfers between devices  27.9 us (43%)
  waiting for transfers between devices  21.1 us (33%)
  Pallas kernels  11 us (17%)
  local copies, waits for them, and re-layouts  2.96 us (5%)
  between operations  0.79 us (1%)
    all_to_all x1, starting transfers between devices, shards(): lax.all_to_all(jnp.broadcast_to(tree_ids, (n_dp, nodes)), 'dp', split_axi...  12 us
    all_to_all x1, waiting for transfers between devices, shards(): lax.all_to_all(rows.reshape(n_dp, 2 * CAP, width // 2), 'dp', split_axis=...  8.33 us
    all_to_all x1, waiting for transfers between devices, shards(): lax.all_to_all(jnp.broadcast_to(tree_ids, (n_dp, nodes)), 'dp', split_axi...  6.95 us
    pallas_call x2, Pallas kernels, load(): pl.pallas_call(functools.partial(load_kernel, len(arrays)), out_shape=tup...  5.17 us
    ppermute x3, waiting for transfers between devices, shards(): lax.ppermute(pairs[j], 'tensor', swap(n_tp, 2 * j))  4.26 us
    ppermute x1, starting transfers between devices, shards(): other = lax.ppermute(mine, 'tensor', swap(n_tp, 1))  4.26 us
    ppermute x3, starting transfers between devices, shards(): lax.ppermute(pairs[j], 'tensor', swap(n_tp, 2 * j))  3.95 us
    all_to_all x1, starting transfers between devices, shards(): lax.all_to_all(rows.reshape(n_dp, 2 * CAP, width // 2), 'dp', split_axis=...  3.85 us
  transfers between devices with their start and end apart: 10, of which 6 were waited for; matrix products, arithmetic and copies ran while one was open for 1% of the time, Pallas kernels for 9%

profile of v2, /device:TPU:1, one launch (start us, length us, event | category | flops | bytes accessed | tf_op | source)
XLA Modules:
  0.0 64.1 jit_solution(14994520951569789324)
XLA Ops:
  0.0 0.0 copy-start.4
  0.0 0.0 copy-start.5
  0.0 0.0 copy-start.3
  0.0 1.3 %broadcast_in_dim.2 = s32[32,1,64]{2,1,0:T(1,128)} broadcast(s32[64]{0:T(128)} %bitcast.16), dimensions={2} | broadcast | bytes 8448 | tf_op jit(solution)/shard_map/broadcast_in_dim | solution.py:200
  1.3 12.0 %all-to-all-start = ((s32[32,1,64]{2,1,0:T(1,128)}), s32[32,1,64]{2,1,0:T(1,128)S(1)}, u32[]{:S(2)}, u32[]{:S(2)}) async-start(s32[32,1,64]{2,1,0:T(1,128)} %broadcast_in_dim.2), calls=%async_computation | async-start | bytes 32768 | tf_op jit(solution)/shard_map/all_to_all | solution.py:199
  13.4 1.6 %load.2.table_ref = bf16[2048,512]{1,0:T(8,128)(2,1)S(1)} custom-call(bf16[2048,512]{1,0:T(8,128)(2,1)} %refs_0_.2), custom_call_target="tpu_custom_call" | custom-call | bytes 2097152 | tf_op jit(solution)/shard_map/load/pallas_call | solution.py:138
  15.0 6.9 %all-to-all-done = s32[32,1,64]{2,1,0:T(1,128)S(1)} async-done(((s32[32,1,64]{2,1,0:T(1,128)}), s32[32,1,64]{2,1,0:T(1,128)S(1)}, u32[]{:S(2)}, u32[]{:S(2)}) %all-to-all-start) | async-done | bytes 8224 | tf_op jit(solution)/shard_map/all_to_all | solution.py:199
  21.9 1.7 %rows.1 = bf16[256,256]{1,0:T(8,128)(2,1)} custom-call(s32[1]{0:T(128)} %bitcast.idx_ref, s32[32,64]{1,0:T(8,128)S(1)} %bitcast.15, bf16[2048,512]{1,0:T(8,128)(2,1)S(1)} %load.2.table_ref), custom_call_target="tpu_custom_call" | custom-call | tf_op jit(solution)/shard_map/rows/pallas_call | solution.py:203
  23.6 3.8 %all-to-all-start.1 = ((bf16[32,8,256]{2,1,0:T(8,128)(2,1)}), bf16[32,8,256]{2,1,0:T(8,128)(2,1)S(1)}, u32[]{:S(2)}, u32[]{:S(2)}) async-start(bf16[32,8,256]{2,1,0:T(8,128)(2,1)} %bitcast.3), calls=%async_computation.1 | async-start | bytes 262144 | tf_op jit(solution)/shard_map/all_to_all | solution.py:211
  28.1 0.0 copy-done.5
  28.2 0.0 copy-done.3
  28.2 0.1 reduce_sum.9
  28.3 8.3 %all-to-all-done.1 = bf16[32,8,256]{2,1,0:T(8,128)(2,1)S(1)} async-done(((bf16[32,8,256]{2,1,0:T(8,128)(2,1)}), bf16[32,8,256]{2,1,0:T(8,128)(2,1)S(1)}, u32[]{:S(2)}, u32[]{:S(2)}) %all-to-all-start.1) | async-done | bytes 131104 | tf_op jit(solution)/shard_map/all_to_all | solution.py:211
  36.6 0.0 copy-done.4
  36.6 0.4 pick.1.refs_3_.refs_0_.emb_ref
  37.0 2.6 %collective-permute-start.2 = (bf16[64,512]{1,0:T(8,128)(2,1)S(1)}, bf16[64,512]{1,0:T(8,128)(2,1)S(1)}, u32[]{:S(2)}, u32[]{:S(2)}) collective-permute-start(bf16[64,512]{1,0:T(8,128)(2,1)S(1)} %pick.1.refs_3_.refs_0_.emb_ref), channel_id=1, source_target_pairs={{0,6},{1,7},{2,4},{3,5},{4,2},{5,3},{6,0},{7,1},{8,14},{9,15},{10,... | collective-permute-start | bytes 196616 | tf_op jit(solution)/shard_map/ppermute | solution.py:231
  39.5 0.5 collective-permute-start.1
  40.1 0.3 collective-permute-start
  40.3 0.0 copy-start
  40.3 1.6 %copy-done = bf16[2,4096,128]{2,1,0:T(8,128)(2,1)S(1)} copy-done((bf16[2,4096,128]{2,1,0:T(8,128)(2,1)S(1)}, bf16[2,4096,128]{2,1,0:T(8,128)(2,1)}, u32[]{:S(2)}) %copy-start) | copy-done | bytes 2097176
  41.9 0.0 copy-start.1
  41.9 0.0 copy-start.2
  41.9 3.6 %load.3 = (bf16[4096,512]{1,0:T(8,128)(2,1)S(1)}, bf16[2,4096,128]{2,1,0:T(8,128)(2,1)S(1)}, bf16[512,4096]{1,0:T(8,128)(2,1)S(1)}) custom-call(bf16[4096,512]{1,0:T(8,128)(2,1)} %refs_0_.3, bf16[2,4096,128]{2,1,0:T(8,128)(2,1)S(1)} %copy-done, bf16[512,4096]{1,0:T(8,128)(2,1)} %refs_2_.1, bf16[64,512]{1,0:T(8,128)(2,1)S(1)} %pick.1.refs_3_.refs_0_.emb_ref), custom_call_target="tpu_custom_call" | custom-call | bytes 10485760 | tf_op jit(solution)/shard_map/load/pallas_call | solution.py:138
  45.5 0.0 collective-permute-done.2.refs_3_
  45.5 0.0 collective-permute-done.1.refs_2_
  45.5 0.0 collective-permute-done.refs_1_
  45.6 4.3 %collective-permute-start.3 = (bf16[4,64,512]{2,1,0:T(8,128)(2,1)S(1)}, bf16[4,64,512]{2,1,0:T(8,128)(2,1)S(1)}, u32[]{:S(2)}, u32[]{:S(2)}) collective-permute-start(bf16[4,64,512]{2,1,0:T(8,128)(2,1)S(1)} %stack.1.mine_ref), channel_id=1, source_target_pairs={{0,1},{1,0},{2,3},{3,2},{4,5},{5,4},{6,7},{7,6},{8,9},{9,8},{10,11... | collective-permute-start | bytes 786440 | tf_op jit(solution)/shard_map/ppermute | solution.py:232
  49.8 0.2 fusion
  50.0 0.1 pad_maximum_fusion
  50.1 0.9 %collective-permute-done.3.other_ref = bf16[4,64,512]{2,1,0:T(8,128)(2,1)S(1)} collective-permute-done((bf16[4,64,512]{2,1,0:T(8,128)(2,1)S(1)}, bf16[4,64,512]{2,1,0:T(8,128)(2,1)S(1)}, u32[]{:S(2)}, u32[]{:S(2)}) %collective-permute-start.3) | collective-permute-done | bytes 262176 | tf_op jit(solution)/shard_map/ppermute | solution.py:232
  51.0 0.0 copy-done.1
  51.0 0.0 copy-done.2
  51.0 2.5 %layer.1 = (bf16[64,512]{1,0:T(8,128)(2,1)S(1)}, bf16[4,64,512]{2,1,0:T(8,128)(2,1)S(1)}) custom-call(s32[1]{0:T(128)} %bitcast.5.idx_ref, s32[1]{0:T(128)} %copy.11.len_ref, bf16[4,64,512]{2,1,0:T(8,128)(2,1)S(1)} %stack.1.mine_ref, bf16[4,64,512]{2,1,0:T(8,128)(2,1)S(1)} %collective-permute-done.3.other_ref, bf16[1,4096]{1,0:T(2,128)(2,1)S(1)} %reshape.35.gain_ref, ...), custom_call_target="tpu_custom_call" | custom-call | tf_op jit(solution)/shard_map/layer/pallas_call | solution.py:244
  53.6 0.5 collective-permute-start.4
  54.0 0.5 project.1.own_ref
  54.5 0.7 %collective-permute-done.4.came_ref = bf16[4,64,512]{2,1,0:T(8,128)(2,1)S(1)} collective-permute-done((bf16[4,64,512]{2,1,0:T(8,128)(2,1)S(1)}, bf16[4,64,512]{2,1,0:T(8,128)(2,1)S(1)}, u32[]{:S(2)}, u32[]{:S(2)}) %collective-permute-start.4) | collective-permute-done | bytes 262176 | tf_op jit(solution)/shard_map/ppermute | solution.py:259
  55.2 1.3 %collective-permute-start.5 = (bf16[64,512]{1,0:T(8,128)(2,1)S(1)}, bf16[64,512]{1,0:T(8,128)(2,1)S(1)}, u32[]{:S(2)}, u32[]{:S(2)}) collective-permute-start(bf16[64,512]{1,0:T(8,128)(2,1)S(1)} %get-tuple-element.20), channel_id=1, source_target_pairs={{0,2},{1,3},{2,0},{3,1},{4,6},{5,7},{6,4},{7,5},{8,10},{9,11},{10,... | collective-permute-start | bytes 196616 | tf_op jit(solution)/shard_map/ppermute | solution.py:279
  56.5 2.5 %collective-permute-start.6 = (bf16[64,512]{1,0:T(8,128)(2,1)S(1)}, bf16[64,512]{1,0:T(8,128)(2,1)S(1)}, u32[]{:S(2)}, u32[]{:S(2)}) collective-permute-start(bf16[64,512]{1,0:T(8,128)(2,1)S(1)} %get-tuple-element.21), channel_id=1, source_target_pairs={{0,4},{1,5},{2,6},{3,7},{4,0},{5,1},{6,2},{7,3},{8,12},{9,13},{10,... | collective-permute-start | bytes 196616 | tf_op jit(solution)/shard_map/ppermute | solution.py:279
  59.0 0.2 collective-permute-start.7
  59.2 0.0 collective-permute-done.5.refs_0_
  59.2 2.7 %collective-permute-done.6.refs_1_ = bf16[64,512]{1,0:T(8,128)(2,1)S(1)} collective-permute-done((bf16[64,512]{1,0:T(8,128)(2,1)S(1)}, bf16[64,512]{1,0:T(8,128)(2,1)S(1)}, u32[]{:S(2)}, u32[]{:S(2)}) %collective-permute-start.6) | collective-permute-done | bytes 65568 | tf_op jit(solution)/shard_map/ppermute | solution.py:279
  61.9 1.5 %collective-permute-done.7.refs_2_ = bf16[64,512]{1,0:T(8,128)(2,1)S(1)} collective-permute-done((bf16[64,512]{1,0:T(8,128)(2,1)S(1)}, bf16[64,512]{1,0:T(8,128)(2,1)S(1)}, u32[]{:S(2)}, u32[]{:S(2)}) %collective-permute-start.7) | collective-permute-done | bytes 65568 | tf_op jit(solution)/shard_map/ppermute | solution.py:279
  63.5 0.7 %final.1 = bf16[64,512]{1,0:T(8,128)(2,1)} custom-call(bf16[64,512]{1,0:T(8,128)(2,1)S(1)} %pick.1.refs_3_.refs_0_.emb_ref, f32[64,512]{1,0:T(8,128)S(1)} %get-tuple-element.19.own_ref, bf16[64,512]{1,0:T(8,128)(2,1)S(1)} %collective-permute-done.5.refs_0_, bf16[64,512]{1,0:T(8,128)(2,1)S(1)} %collective-permute-done.6.refs_1_, ...), custom_call_target="tpu_custom_call" | custom-call | tf_op jit(solution)/shard_map/final/pallas_call | solution.py:280
  (5 shorter events, 0.1 us)
Async XLA Ops:
  0.0 36.6 %copy-start.4 = (s32[1,64]{1,0:T(1,128)S(1)}, s32[1,64]{1,0:T(1,128)}, u32[]{:S(2)}) copy-start(s32[1,64]{1,0:T(1,128)} %ids_ref.1) | copy-start | bytes 772
  0.0 28.1 %copy-start.5 = (bf16[4096]{0:T(1024)(128)(2,1)S(1)}, bf16[4096]{0:T(1024)(128)(2,1)}, u32[]{:S(2)}) copy-start(bf16[4096]{0:T(1024)(128)(2,1)} %param.14) | copy-start | bytes 24580
  0.0 28.1 %copy-start.3 = (s32[1,64,64]{2,1,0:T(8,128)S(1)}, s32[1,64,64]{2,1,0:T(8,128)}, u32[]{:S(2)}) copy-start(s32[1,64,64]{2,1,0:T(8,128)} %param.11) | copy-start | bytes 49156
  1.3 20.6 %all-to-all-start = ((s32[32,1,64]{2,1,0:T(1,128)}), s32[32,1,64]{2,1,0:T(1,128)S(1)}, u32[]{:S(2)}, u32[]{:S(2)}) async-start(s32[32,1,64]{2,1,0:T(1,128)} %broadcast_in_dim.2), calls=%async_computation | async-start | bytes 32768 | tf_op jit(solution)/shard_map/all_to_all | solution.py:199
  23.6 13.0 %all-to-all-start.1 = ((bf16[32,8,256]{2,1,0:T(8,128)(2,1)}), bf16[32,8,256]{2,1,0:T(8,128)(2,1)S(1)}, u32[]{:S(2)}, u32[]{:S(2)}) async-start(bf16[32,8,256]{2,1,0:T(8,128)(2,1)} %bitcast.3), calls=%async_computation.1 | async-start | bytes 262144 | tf_op jit(solution)/shard_map/all_to_all | solution.py:211
  37.0 8.5 %collective-permute-start.2 = (bf16[64,512]{1,0:T(8,128)(2,1)S(1)}, bf16[64,512]{1,0:T(8,128)(2,1)S(1)}, u32[]{:S(2)}, u32[]{:S(2)}) collective-permute-start(bf16[64,512]{1,0:T(8,128)(2,1)S(1)} %pick.1.refs_3_.refs_0_.emb_ref), channel_id=1, source_target_pairs={{0,6},{1,7},{2,4},{3,5},{4,2},{5,3},{6,0},{7,1},{8,14},{9,15},{10,... | collective-permute-start | bytes 196616 | tf_op jit(solution)/shard_map/ppermute | solution.py:231
  39.5 6.0 %collective-permute-start.1 = (bf16[64,512]{1,0:T(8,128)(2,1)S(1)}, bf16[64,512]{1,0:T(8,128)(2,1)S(1)}, u32[]{:S(2)}, u32[]{:S(2)}) collective-permute-start(bf16[64,512]{1,0:T(8,128)(2,1)S(1)} %pick.1.refs_3_.refs_0_.emb_ref), channel_id=1, source_target_pairs={{0,4},{1,5},{2,6},{3,7},{4,0},{5,1},{6,2},{7,3},{8,12},{9,13},{10,... | collective-permute-start | bytes 196616 | tf_op jit(solution)/shard_map/ppermute | solution.py:231
  40.1 5.5 %collective-permute-start = (bf16[64,512]{1,0:T(8,128)(2,1)S(1)}, bf16[64,512]{1,0:T(8,128)(2,1)S(1)}, u32[]{:S(2)}, u32[]{:S(2)}) collective-permute-start(bf16[64,512]{1,0:T(8,128)(2,1)S(1)} %pick.1.refs_3_.refs_0_.emb_ref), channel_id=1, source_target_pairs={{0,2},{1,3},{2,0},{3,1},{4,6},{5,7},{6,4},{7,5},{8,10},{9,11},{10,... | collective-permute-start | bytes 196616 | tf_op jit(solution)/shard_map/ppermute | solution.py:231
  40.3 1.6 %copy-start = (bf16[2,4096,128]{2,1,0:T(8,128)(2,1)S(1)}, bf16[2,4096,128]{2,1,0:T(8,128)(2,1)}, u32[]{:S(2)}) copy-start(bf16[2,4096,128]{2,1,0:T(8,128)(2,1)} %refs_1_.1) | copy-start | bytes 6291460
  41.9 9.1 %copy-start.1 = (bf16[1,1,1024,128]{3,2,1,0:T(8,128)(2,1)S(1)}, bf16[1,1,1024,128]{3,2,1,0:T(8,128)(2,1)}, u32[]{:S(2)}) copy-start(bf16[1,1,1024,128]{3,2,1,0:T(8,128)(2,1)} %param.18) | copy-start | bytes 786436
  41.9 9.1 %copy-start.2 = (bf16[1,1,1024,128]{3,2,1,0:T(8,128)(2,1)S(1)}, bf16[1,1,1024,128]{3,2,1,0:T(8,128)(2,1)}, u32[]{:S(2)}) copy-start(bf16[1,1,1024,128]{3,2,1,0:T(8,128)(2,1)} %param.19) | copy-start | bytes 786436
  45.6 5.4 %collective-permute-start.3 = (bf16[4,64,512]{2,1,0:T(8,128)(2,1)S(1)}, bf16[4,64,512]{2,1,0:T(8,128)(2,1)S(1)}, u32[]{:S(2)}, u32[]{:S(2)}) collective-permute-start(bf16[4,64,512]{2,1,0:T(8,128)(2,1)S(1)} %stack.1.mine_ref), channel_id=1, source_target_pairs={{0,1},{1,0},{2,3},{3,2},{4,5},{5,4},{6,7},{7,6},{8,9},{9,8},{10,11... | collective-permute-start | bytes 786440 | tf_op jit(solution)/shard_map/ppermute | solution.py:232
  53.6 1.6 %collective-permute-start.4 = (bf16[4,64,512]{2,1,0:T(8,128)(2,1)S(1)}, bf16[4,64,512]{2,1,0:T(8,128)(2,1)S(1)}, u32[]{:S(2)}, u32[]{:S(2)}) collective-permute-start(bf16[4,64,512]{2,1,0:T(8,128)(2,1)S(1)} %get-tuple-element.18), channel_id=1, source_target_pairs={{0,1},{1,0},{2,3},{3,2},{4,5},{5,4},{6,7},{7,6},{8,9},{9,8},{10,11... | collective-permute-start | bytes 786440 | tf_op jit(solution)/shard_map/ppermute | solution.py:259
  55.2 3.9 %collective-permute-start.5 = (bf16[64,512]{1,0:T(8,128)(2,1)S(1)}, bf16[64,512]{1,0:T(8,128)(2,1)S(1)}, u32[]{:S(2)}, u32[]{:S(2)}) collective-permute-start(bf16[64,512]{1,0:T(8,128)(2,1)S(1)} %get-tuple-element.20), channel_id=1, source_target_pairs={{0,2},{1,3},{2,0},{3,1},{4,6},{5,7},{6,4},{7,5},{8,10},{9,11},{10,... | collective-permute-start | bytes 196616 | tf_op jit(solution)/shard_map/ppermute | solution.py:279
  56.5 5.4 %collective-permute-start.6 = (bf16[64,512]{1,0:T(8,128)(2,1)S(1)}, bf16[64,512]{1,0:T(8,128)(2,1)S(1)}, u32[]{:S(2)}, u32[]{:S(2)}) collective-permute-start(bf16[64,512]{1,0:T(8,128)(2,1)S(1)} %get-tuple-element.21), channel_id=1, source_target_pairs={{0,4},{1,5},{2,6},{3,7},{4,0},{5,1},{6,2},{7,3},{8,12},{9,13},{10,... | collective-permute-start | bytes 196616 | tf_op jit(solution)/shard_map/ppermute | solution.py:279
  59.0 4.5 %collective-permute-start.7 = (bf16[64,512]{1,0:T(8,128)(2,1)S(1)}, bf16[64,512]{1,0:T(8,128)(2,1)S(1)}, u32[]{:S(2)}, u32[]{:S(2)}) collective-permute-start(bf16[64,512]{1,0:T(8,128)(2,1)S(1)} %get-tuple-element.22), channel_id=1, source_target_pairs={{0,6},{1,7},{2,4},{3,5},{4,2},{5,3},{6,0},{7,1},{8,14},{9,15},{10,... | collective-permute-start | bytes 196616 | tf_op jit(solution)/shard_map/ppermute | solution.py:279

commit v3 on v2

--- a/solution.py
+++ b/solution.py
@@ -31,9 +31,9 @@
     rank = jnp.dot(jnp.where(owned, 1.0, 0.0).astype(BF), before, preferred_element_type=F32)
     high = jnp.where(owned, rank * (vocab // 256) + (off >> 8).astype(F32), -1.0).astype(BF)
     low = jnp.where(owned, (off & 255).astype(F32), 0.0).astype(BF)
-    n_out = n_dst * 2 * CAP
+    n_out = n_dst * CAP
     spread = jnp.where(
-        (iota((n_out, n_dst), 0) >> 3) == iota((n_out, n_dst), 1), 1.0, 0.0
+        iota((n_out, n_dst), 0) // CAP == iota((n_out, n_dst), 1), 1.0, 0.0
     ).astype(BF)
     code = 256.0 * jnp.dot(spread, high, preferred_element_type=F32) + jnp.dot(
         spread, low, preferred_element_type=F32
@@ -47,11 +47,14 @@
     pick = jnp.where(iota((n_out, vocab), 1) == entry, 1.0, 0.0).astype(BF)
     rows = jnp.dot(pick, table_ref[...], preferred_element_type=F32)
     half = rows.shape[1] // 2
-    upper = (iota((n_out, half), 0) & CAP) > 0
-    out_ref[...] = jnp.where(upper, rows[:, half:], rows[:, :half]).astype(BF)
-
-
-def pick_kernel(ids_ref, recv_ref, out_ref, *, vocab):
+    low_half = rows[:, :half].reshape(n_dst // 2, 2 * CAP, half)
+    high_half = rows[:, half:].reshape(n_dst // 2, 2 * CAP, half)
+    first = iota(low_half.shape, 1) < CAP
+    out_ref[:, 0] = jnp.where(first, low_half, pltpu.roll(high_half, CAP, 1)).astype(BF)
+    out_ref[:, 1] = jnp.where(first, pltpu.roll(low_half, CAP, 1), high_half).astype(BF)
+
+
+def pick_kernel(ids_ref, recv_ref, _, out_ref, *, vocab):
     nodes = ids_ref.shape[1]
     n_in, half = recv_ref.shape
     ids_row = jnp.broadcast_to(ids_ref[...], (nodes, nodes)) // vocab
@@ -125,6 +128,10 @@
         send_ref[j] = jnp.dot(ctx, wout_ref[:, cols], preferred_element_type=F32).astype(BF)
 
 
+def spread_kernel(ids_ref, out_ref):
+    out_ref[...] = jnp.broadcast_to(ids_ref[...], out_ref.shape)
+
+
 def load_kernel(count, *refs):
     dst = refs[-1 - count : -1]
     copies = [pltpu.make_async_copy(refs[i], dst[i], refs[-1].at[i]) for i in range(count)]
@@ -196,31 +203,38 @@
     vmem = pl.BlockSpec(memory_space=pltpu.VMEM)
     smem = pl.BlockSpec(memory_space=pltpu.SMEM)
 
-    all_ids = lax.all_to_all(
-        jnp.broadcast_to(tree_ids, (n_dp, nodes)), "dp", split_axis=0, concat_axis=0, tiled=True
-    )
+    copies = pl.pallas_call(
+        spread_kernel,
+        out_shape=jax.ShapeDtypeStruct((n_dp, nodes), jnp.int32),
+        in_specs=[vmem],
+        out_specs=vmem,
+        compiler_params=limit(60),
+        name="spread",
+    )(tree_ids)
+    all_ids = lax.all_to_all(copies, "dp", split_axis=0, concat_axis=0, tiled=True)
     (table_held,) = load((table,), (), 50)
     rows = pl.pallas_call(
         rows_kernel,
-        out_shape=jax.ShapeDtypeStruct((n_dp * 2 * CAP, width // 2), BF),
+        out_shape=jax.ShapeDtypeStruct((n_dp // 2, 2, 2 * CAP, width // 2), BF),
         in_specs=[smem, vmem, vmem],
         out_specs=vmem,
         compiler_params=limit(12),
         name="rows",
     )(part, all_ids, table_held)
+    w_kv, key_cache, value_cache = load((w_kv, key_cache, value_cache), (rows,), 50)
     recv = lax.all_to_all(
         rows.reshape(n_dp, 2 * CAP, width // 2), "dp", split_axis=0, concat_axis=0, tiled=True
     )
     emb = pl.pallas_call(
         functools.partial(pick_kernel, vocab=vocab),
         out_shape=jax.ShapeDtypeStruct((nodes, width), BF),
-        in_specs=[vmem, vmem],
+        in_specs=[vmem, vmem, pl.BlockSpec(memory_space=pl.ANY)],
         out_specs=vmem,
         compiler_params=limit(4),
         name="pick",
-    )(tree_ids, recv.reshape(n_dp * 2 * CAP, width // 2))
-
-    w_query, w_kv, w_out = load((w_query, w_kv, w_out), (emb,), 41)
+    )(tree_ids, recv.reshape(n_dp * 2 * CAP, width // 2), w_kv)
+
+    w_query, w_out = load((w_query, w_out), (emb,), 45)
     mine = pl.pallas_call(
         stack_kernel,
         in_specs=[vmem] * n_x + [pl.BlockSpec(memory_space=pl.ANY)],
@@ -228,7 +242,7 @@
         out_shape=jax.ShapeDtypeStruct((n_x, nodes, width), BF),
         compiler_params=limit(4),
         name="stack",
-    )(emb, *[lax.ppermute(emb, "tensor", swap(n_tp, 2 * j)) for j in range(1, n_x)], w_kv)
+    )(emb, *[lax.ppermute(emb, "tensor", swap(n_tp, 2 * j)) for j in range(1, n_x)], w_query)
     other = lax.ppermute(mine, "tensor", swap(n_tp, 1))
 
     depth = jnp.sum(ancestors[0], axis=1) - 1

time: 64.4 us -> 62.5 us (0.970)
  local copies, waits for them, and re-layouts: 2.96 us -> 0.03 us
  Pallas kernels: 11 us -> 13.6 us
  waiting for transfers between devices: 21.1 us -> 18.9 us
    all_to_all x1, waiting for transfers between devices: 8.33 us -> 6.68 us  [shards(): lax.all_to_all(rows.reshape(n_dp, 2 * CAP, width // 2), 'dp', split_axis=...]
    unnamed x12 -> x10, local copies, waits for them, and re-layouts: 1.61 us -> 0.02 us
    pallas_call x2 -> x3, Pallas kernels: 5.17 us -> 6.72 us  [load(): pl.pallas_call(functools.partial(load_kernel, len(arrays)), out_shape=tup...]
    broadcast_in_dim x1 -> x0, local copies, waits for them, and re-layouts: 1.33 us -> none  [shards(): jnp.broadcast_to(tree_ids, (n_dp, nodes))]
    pallas_call x1 -> x2, Pallas kernels: 1.67 us -> 2.75 us  [the longest x1 1.43 us: shards(): pl.pallas_call(rows_kernel, out_shape=jax.ShapeDtypeStruct((n_dp // 2, 2,...]
    ppermute x3, waiting for transfers between devices: 4.26 us -> 3.36 us  [shards(): lax.ppermute(pairs[j], 'tensor', swap(n_tp, 2 * j))]
  transfers between devices with their start and end apart: 10 -> 10, of which waited for: 6 -> 7; matrix products, arithmetic and copies ran while one was open for 1% -> 1% of each run, Pallas kernels for 9% -> 12%
where the time goes in v3:
time: 62.5 us; the launch traced here: 62.2 us
  starting transfers between devices  28.5 us (46%)
  waiting for transfers between devices  18.9 us (30%)
  Pallas kernels  13.6 us (22%)
  between operations  0.81 us (1%)
    all_to_all x1, starting transfers between devices, shards(): lax.all_to_all(copies, 'dp', split_axis=0, concat_axis=0, tiled=True)  12 us
    all_to_all x1, waiting for transfers between devices, shards(): lax.all_to_all(copies, 'dp', split_axis=0, concat_axis=0, tiled=True)  6.93 us
    pallas_call x3, Pallas kernels, load(): pl.pallas_call(functools.partial(load_kernel, len(arrays)), out_shape=tup...  6.72 us
    all_to_all x1, waiting for transfers between devices, shards(): lax.all_to_all(rows.reshape(n_dp, 2 * CAP, width // 2), 'dp', split_axis=...  6.68 us
    ppermute x1, starting transfers between devices, shards(): other = lax.ppermute(mine, 'tensor', swap(n_tp, 1))  4.85 us
    ppermute x3, starting transfers between devices, shards(): lax.ppermute(pairs[j], 'tensor', swap(n_tp, 2 * j))  3.95 us
    all_to_all x1, starting transfers between devices, shards(): lax.all_to_all(rows.reshape(n_dp, 2 * CAP, width // 2), 'dp', split_axis=...  3.85 us
    ppermute x3, waiting for transfers between devices, shards(): lax.ppermute(pairs[j], 'tensor', swap(n_tp, 2 * j))  3.36 us
  transfers between devices with their start and end apart: 10, of which 7 were waited for; matrix products, arithmetic and copies ran while one was open for 1% of the time, Pallas kernels for 12%

profile of v3, /device:TPU:1, one launch (start us, length us, event | category | flops | bytes accessed | tf_op | source)
XLA Modules:
  0.0 62.2 jit_solution(15683968545558767522)
XLA Ops:
  0.0 0.0 copy-start.4
  0.0 0.0 copy-start.2
  0.0 0.0 copy-start.1
  0.0 0.0 copy-start
  0.0 1.3 %spread.1 = s32[32,64]{1,0:T(8,128)} custom-call(s32[1,64]{1,0:T(1,128)} %ids_ref.3), custom_call_target="tpu_custom_call" | custom-call | tf_op jit(solution)/shard_map/spread/pallas_call | solution.py:206
  1.3 12.0 %all-to-all-start = ((s32[32,1,64]{2,1,0:T(1,128)}), s32[32,1,64]{2,1,0:T(1,128)S(1)}, u32[]{:S(2)}, u32[]{:S(2)}) async-start(s32[32,1,64]{2,1,0:T(1,128)} %bitcast.18), calls=%async_computation | async-start | bytes 32768 | tf_op jit(solution)/shard_map/all_to_all | solution.py:214
  13.4 0.0 copy-start.3
  13.4 1.6 %load.3.table_ref = bf16[2048,512]{1,0:T(8,128)(2,1)S(1)} custom-call(bf16[2048,512]{1,0:T(8,128)(2,1)} %refs_0_.3), custom_call_target="tpu_custom_call" | custom-call | bytes 2097152 | tf_op jit(solution)/shard_map/load/pallas_call | solution.py:145
  15.0 6.9 %all-to-all-done = s32[32,1,64]{2,1,0:T(1,128)S(1)} async-done(((s32[32,1,64]{2,1,0:T(1,128)}), s32[32,1,64]{2,1,0:T(1,128)S(1)}, u32[]{:S(2)}, u32[]{:S(2)}) %all-to-all-start) | async-done | bytes 8224 | tf_op jit(solution)/shard_map/all_to_all | solution.py:214
  21.9 1.4 %rows.1.refs_3_ = bf16[16,2,8,256]{3,2,1,0:T(8,128)(2,1)} custom-call(s32[1]{0:T(128)} %bitcast.idx_ref, s32[32,64]{1,0:T(8,128)S(1)} %bitcast.17, bf16[2048,512]{1,0:T(8,128)(2,1)S(1)} %load.3.table_ref), custom_call_target="tpu_custom_call" | custom-call | tf_op jit(solution)/shard_map/rows/pallas_call | solution.py:216
  23.4 3.9 %all-to-all-start.1 = ((bf16[32,8,256]{2,1,0:T(8,128)(2,1)}), bf16[32,8,256]{2,1,0:T(8,128)(2,1)S(1)}, u32[]{:S(2)}, u32[]{:S(2)}) async-start(bf16[32,8,256]{2,1,0:T(8,128)(2,1)} %bitcast.4), calls=%async_computation.1 | async-start | bytes 262144 | tf_op jit(solution)/shard_map/all_to_all | solution.py:225
  27.9 0.0 copy-done.4
  27.9 0.0 copy-done.2
  27.9 0.1 reduce_sum.9
  28.0 0.0 copy-done.1
  28.1 0.0 copy-done
  28.1 1.6 %load.4 = (bf16[2,4096,128]{2,1,0:T(8,128)(2,1)S(1)}, bf16[1,1,1024,128]{3,2,1,0:T(8,128)(2,1)S(1)}, bf16[1,1,1024,128]{3,2,1,0:T(8,128)(2,1)S(1)}) custom-call(bf16[2,4096,128]{2,1,0:T(8,128)(2,1)} %refs_0_.4, bf16[1,1,1024,128]{3,2,1,0:T(8,128)(2,1)S(1)} %copy-done, bf16[1,1,1024,128]{3,2,1,0:T(8,128)(2,1)S(1)} %copy-done.1, ...), custom_call_target="tpu_custom_call" | custom-call | bytes 2621440 | tf_op jit(solution)/shard_map/load/pallas_call | solution.py:145
  29.7 6.7 %all-to-all-done.1 = bf16[32,8,256]{2,1,0:T(8,128)(2,1)S(1)} async-done(((bf16[32,8,256]{2,1,0:T(8,128)(2,1)}), bf16[32,8,256]{2,1,0:T(8,128)(2,1)S(1)}, u32[]{:S(2)}, u32[]{:S(2)}) %all-to-all-start.1) | async-done | bytes 131104 | tf_op jit(solution)/shard_map/all_to_all | solution.py:225
  36.4 0.0 copy-done.3
  36.4 0.4 pick.1.refs_2_.refs_0_.emb_ref
  36.7 2.6 %collective-permute-start.2 = (bf16[64,512]{1,0:T(8,128)(2,1)S(1)}, bf16[64,512]{1,0:T(8,128)(2,1)S(1)}, u32[]{:S(2)}, u32[]{:S(2)}) collective-permute-start(bf16[64,512]{1,0:T(8,128)(2,1)S(1)} %pick.1.refs_2_.refs_0_.emb_ref), channel_id=1, source_target_pairs={{0,6},{1,7},{2,4},{3,5},{4,2},{5,3},{6,0},{7,1},{8,14},{9,15},{10,... | collective-permute-start | bytes 196616 | tf_op jit(solution)/shard_map/ppermute | solution.py:245
  39.3 0.5 collective-permute-start.1
  39.8 0.3 collective-permute-start
  40.1 3.5 %load.5 = (bf16[4096,512]{1,0:T(8,128)(2,1)S(1)}, bf16[512,4096]{1,0:T(8,128)(2,1)S(1)}) custom-call(bf16[4096,512]{1,0:T(8,128)(2,1)} %refs_0_.5, bf16[512,4096]{1,0:T(8,128)(2,1)} %refs_1_.3, bf16[64,512]{1,0:T(8,128)(2,1)S(1)} %pick.1.refs_2_.refs_0_.emb_ref), custom_call_target="tpu_custom_call" | custom-call | bytes 8388608 | tf_op jit(solution)/shard_map/load/pallas_call | solution.py:145
  43.6 0.0 collective-permute-done.2.refs_3_
  43.6 0.3 collective-permute-done.1.refs_2_
  43.9 0.0 collective-permute-done.refs_1_
  44.0 4.8 %collective-permute-start.3 = (bf16[4,64,512]{2,1,0:T(8,128)(2,1)S(1)}, bf16[4,64,512]{2,1,0:T(8,128)(2,1)S(1)}, u32[]{:S(2)}, u32[]{:S(2)}) collective-permute-start(bf16[4,64,512]{2,1,0:T(8,128)(2,1)S(1)} %stack.1.mine_ref), channel_id=1, source_target_pairs={{0,1},{1,0},{2,3},{3,2},{4,5},{5,4},{6,7},{7,6},{8,9},{9,8},{10,11... | collective-permute-start | bytes 786440 | tf_op jit(solution)/shard_map/ppermute | solution.py:246
  48.8 0.2 fusion
  49.0 0.1 pad_maximum_fusion
  49.1 0.9 %collective-permute-done.3.other_ref = bf16[4,64,512]{2,1,0:T(8,128)(2,1)S(1)} collective-permute-done((bf16[4,64,512]{2,1,0:T(8,128)(2,1)S(1)}, bf16[4,64,512]{2,1,0:T(8,128)(2,1)S(1)}, u32[]{:S(2)}, u32[]{:S(2)}) %collective-permute-start.3) | collective-permute-done | bytes 262176 | tf_op jit(solution)/shard_map/ppermute | solution.py:246
  50.0 2.5 %layer.1 = (bf16[64,512]{1,0:T(8,128)(2,1)S(1)}, bf16[4,64,512]{2,1,0:T(8,128)(2,1)S(1)}) custom-call(s32[1]{0:T(128)} %bitcast.6.idx_ref, s32[1]{0:T(128)} %copy.12.len_ref, bf16[4,64,512]{2,1,0:T(8,128)(2,1)S(1)} %stack.1.mine_ref, bf16[4,64,512]{2,1,0:T(8,128)(2,1)S(1)} %collective-permute-done.3.other_ref, bf16[1,4096]{1,0:T(2,128)(2,1)S(1)} %reshape.31.gain_ref, ...), custom_call_target="tpu_custom_call" | custom-call | tf_op jit(solution)/shard_map/layer/pallas_call | solution.py:258
  52.5 0.5 collective-permute-start.4
  53.0 0.5 project.1.own_ref
  53.5 0.7 %collective-permute-done.4.came_ref = bf16[4,64,512]{2,1,0:T(8,128)(2,1)S(1)} collective-permute-done((bf16[4,64,512]{2,1,0:T(8,128)(2,1)S(1)}, bf16[4,64,512]{2,1,0:T(8,128)(2,1)S(1)}, u32[]{:S(2)}, u32[]{:S(2)}) %collective-permute-start.4) | collective-permute-done | bytes 262176 | tf_op jit(solution)/shard_map/ppermute | solution.py:273
  54.2 0.4 collective-permute-start.5
  54.6 2.4 %collective-permute-start.6 = (bf16[64,512]{1,0:T(8,128)(2,1)S(1)}, bf16[64,512]{1,0:T(8,128)(2,1)S(1)}, u32[]{:S(2)}, u32[]{:S(2)}) collective-permute-start(bf16[64,512]{1,0:T(8,128)(2,1)S(1)} %get-tuple-element.25), channel_id=1, source_target_pairs={{0,4},{1,5},{2,6},{3,7},{4,0},{5,1},{6,2},{7,3},{8,12},{9,13},{10,... | collective-permute-start | bytes 196616 | tf_op jit(solution)/shard_map/ppermute | solution.py:293
  57.1 1.1 %collective-permute-start.7 = (bf16[64,512]{1,0:T(8,128)(2,1)S(1)}, bf16[64,512]{1,0:T(8,128)(2,1)S(1)}, u32[]{:S(2)}, u32[]{:S(2)}) collective-permute-start(bf16[64,512]{1,0:T(8,128)(2,1)S(1)} %get-tuple-element.26), channel_id=1, source_target_pairs={{0,6},{1,7},{2,4},{3,5},{4,2},{5,3},{6,0},{7,1},{8,14},{9,15},{10,... | collective-permute-start | bytes 196616 | tf_op jit(solution)/shard_map/ppermute | solution.py:293
  58.2 0.0 collective-permute-done.5.refs_0_
  58.2 1.8 %collective-permute-done.6.refs_1_ = bf16[64,512]{1,0:T(8,128)(2,1)S(1)} collective-permute-done((bf16[64,512]{1,0:T(8,128)(2,1)S(1)}, bf16[64,512]{1,0:T(8,128)(2,1)S(1)}, u32[]{:S(2)}, u32[]{:S(2)}) %collective-permute-start.6) | collective-permute-done | bytes 65568 | tf_op jit(solution)/shard_map/ppermute | solution.py:293
  60.0 1.5 %collective-permute-done.7.refs_2_ = bf16[64,512]{1,0:T(8,128)(2,1)S(1)} collective-permute-done((bf16[64,512]{1,0:T(8,128)(2,1)S(1)}, bf16[64,512]{1,0:T(8,128)(2,1)S(1)}, u32[]{:S(2)}, u32[]{:S(2)}) %collective-permute-start.7) | collective-permute-done | bytes 65568 | tf_op jit(solution)/shard_map/ppermute | solution.py:293
  61.5 0.7 %final.1 = bf16[64,512]{1,0:T(8,128)(2,1)} custom-call(bf16[64,512]{1,0:T(8,128)(2,1)S(1)} %pick.1.refs_2_.refs_0_.emb_ref, f32[64,512]{1,0:T(8,128)S(1)} %get-tuple-element.23.own_ref, bf16[64,512]{1,0:T(8,128)(2,1)S(1)} %collective-permute-done.5.refs_0_, bf16[64,512]{1,0:T(8,128)(2,1)S(1)} %collective-permute-done.6.refs_1_, ...), custom_call_target="tpu_custom_call" | custom-call | tf_op jit(solution)/shard_map/final/pallas_call | solution.py:294
  (5 shorter events, 0.1 us)
Async XLA Ops:
  0.0 27.9 %copy-start.4 = (bf16[4096]{0:T(1024)(128)(2,1)S(1)}, bf16[4096]{0:T(1024)(128)(2,1)}, u32[]{:S(2)}) copy-start(bf16[4096]{0:T(1024)(128)(2,1)} %param.14) | copy-start | bytes 24580
  0.0 27.9 %copy-start.2 = (s32[1,64,64]{2,1,0:T(8,128)S(1)}, s32[1,64,64]{2,1,0:T(8,128)}, u32[]{:S(2)}) copy-start(s32[1,64,64]{2,1,0:T(8,128)} %param.11) | copy-start | bytes 49156
  0.0 28.0 %copy-start.1 = (bf16[1,1,1024,128]{3,2,1,0:T(8,128)(2,1)S(1)}, bf16[1,1,1024,128]{3,2,1,0:T(8,128)(2,1)}, u32[]{:S(2)}) copy-start(bf16[1,1,1024,128]{3,2,1,0:T(8,128)(2,1)} %refs_2_.1) | copy-start | bytes 786436
  0.0 28.0 %copy-start = (bf16[1,1,1024,128]{3,2,1,0:T(8,128)(2,1)S(1)}, bf16[1,1,1024,128]{3,2,1,0:T(8,128)(2,1)}, u32[]{:S(2)}) copy-start(bf16[1,1,1024,128]{3,2,1,0:T(8,128)(2,1)} %refs_1_.2) | copy-start | bytes 786436
  1.3 20.6 %all-to-all-start = ((s32[32,1,64]{2,1,0:T(1,128)}), s32[32,1,64]{2,1,0:T(1,128)S(1)}, u32[]{:S(2)}, u32[]{:S(2)}) async-start(s32[32,1,64]{2,1,0:T(1,128)} %bitcast.18), calls=%async_computation | async-start | bytes 32768 | tf_op jit(solution)/shard_map/all_to_all | solution.py:214
  13.4 23.0 %copy-start.3 = (s32[1,64]{1,0:T(1,128)S(1)}, s32[1,64]{1,0:T(1,128)}, u32[]{:S(2)}) copy-start(s32[1,64]{1,0:T(1,128)} %ids_ref.3) | copy-start | bytes 772
  23.4 13.0 %all-to-all-start.1 = ((bf16[32,8,256]{2,1,0:T(8,128)(2,1)}), bf16[32,8,256]{2,1,0:T(8,128)(2,1)S(1)}, u32[]{:S(2)}, u32[]{:S(2)}) async-start(bf16[32,8,256]{2,1,0:T(8,128)(2,1)} %bitcast.4), calls=%async_computation.1 | async-start | bytes 262144 | tf_op jit(solution)/shard_map/all_to_all | solution.py:225
  36.7 6.8 %collective-permute-start.2 = (bf16[64,512]{1,0:T(8,128)(2,1)S(1)}, bf16[64,512]{1,0:T(8,128)(2,1)S(1)}, u32[]{:S(2)}, u32[]{:S(2)}) collective-permute-start(bf16[64,512]{1,0:T(8,128)(2,1)S(1)} %pick.1.refs_2_.refs_0_.emb_ref), channel_id=1, source_target_pairs={{0,6},{1,7},{2,4},{3,5},{4,2},{5,3},{6,0},{7,1},{8,14},{9,15},{10,... | collective-permute-start | bytes 196616 | tf_op jit(solution)/shard_map/ppermute | solution.py:245
  39.3 4.6 %collective-permute-start.1 = (bf16[64,512]{1,0:T(8,128)(2,1)S(1)}, bf16[64,512]{1,0:T(8,128)(2,1)S(1)}, u32[]{:S(2)}, u32[]{:S(2)}) collective-permute-start(bf16[64,512]{1,0:T(8,128)(2,1)S(1)} %pick.1.refs_2_.refs_0_.emb_ref), channel_id=1, source_target_pairs={{0,4},{1,5},{2,6},{3,7},{4,0},{5,1},{6,2},{7,3},{8,12},{9,13},{10,... | collective-permute-start | bytes 196616 | tf_op jit(solution)/shard_map/ppermute | solution.py:245
  39.8 4.1 %collective-permute-start = (bf16[64,512]{1,0:T(8,128)(2,1)S(1)}, bf16[64,512]{1,0:T(8,128)(2,1)S(1)}, u32[]{:S(2)}, u32[]{:S(2)}) collective-permute-start(bf16[64,512]{1,0:T(8,128)(2,1)S(1)} %pick.1.refs_2_.refs_0_.emb_ref), channel_id=1, source_target_pairs={{0,2},{1,3},{2,0},{3,1},{4,6},{5,7},{6,4},{7,5},{8,10},{9,11},{10,... | collective-permute-start | bytes 196616 | tf_op jit(solution)/shard_map/ppermute | solution.py:245
  44.0 6.0 %collective-permute-start.3 = (bf16[4,64,512]{2,1,0:T(8,128)(2,1)S(1)}, bf16[4,64,512]{2,1,0:T(8,128)(2,1)S(1)}, u32[]{:S(2)}, u32[]{:S(2)}) collective-permute-start(bf16[4,64,512]{2,1,0:T(8,128)(2,1)S(1)} %stack.1.mine_ref), channel_id=1, source_target_pairs={{0,1},{1,0},{2,3},{3,2},{4,5},{5,4},{6,7},{7,6},{8,9},{9,8},{10,11... | collective-permute-start | bytes 786440 | tf_op jit(solution)/shard_map/ppermute | solution.py:246
  52.5 1.6 %collective-permute-start.4 = (bf16[4,64,512]{2,1,0:T(8,128)(2,1)S(1)}, bf16[4,64,512]{2,1,0:T(8,128)(2,1)S(1)}, u32[]{:S(2)}, u32[]{:S(2)}) collective-permute-start(bf16[4,64,512]{2,1,0:T(8,128)(2,1)S(1)} %get-tuple-element.22), channel_id=1, source_target_pairs={{0,1},{1,0},{2,3},{3,2},{4,5},{5,4},{6,7},{7,6},{8,9},{9,8},{10,11... | collective-permute-start | bytes 786440 | tf_op jit(solution)/shard_map/ppermute | solution.py:273
  54.2 3.9 %collective-permute-start.5 = (bf16[64,512]{1,0:T(8,128)(2,1)S(1)}, bf16[64,512]{1,0:T(8,128)(2,1)S(1)}, u32[]{:S(2)}, u32[]{:S(2)}) collective-permute-start(bf16[64,512]{1,0:T(8,128)(2,1)S(1)} %get-tuple-element.24), channel_id=1, source_target_pairs={{0,2},{1,3},{2,0},{3,1},{4,6},{5,7},{6,4},{7,5},{8,10},{9,11},{10,... | collective-permute-start | bytes 196616 | tf_op jit(solution)/shard_map/ppermute | solution.py:293
  54.6 5.4 %collective-permute-start.6 = (bf16[64,512]{1,0:T(8,128)(2,1)S(1)}, bf16[64,512]{1,0:T(8,128)(2,1)S(1)}, u32[]{:S(2)}, u32[]{:S(2)}) collective-permute-start(bf16[64,512]{1,0:T(8,128)(2,1)S(1)} %get-tuple-element.25), channel_id=1, source_target_pairs={{0,4},{1,5},{2,6},{3,7},{4,0},{5,1},{6,2},{7,3},{8,12},{9,13},{10,... | collective-permute-start | bytes 196616 | tf_op jit(solution)/shard_map/ppermute | solution.py:293
  57.1 4.5 %collective-permute-start.7 = (bf16[64,512]{1,0:T(8,128)(2,1)S(1)}, bf16[64,512]{1,0:T(8,128)(2,1)S(1)}, u32[]{:S(2)}, u32[]{:S(2)}) collective-permute-start(bf16[64,512]{1,0:T(8,128)(2,1)S(1)} %get-tuple-element.26), channel_id=1, source_target_pairs={{0,6},{1,7},{2,4},{3,5},{4,2},{5,3},{6,0},{7,1},{8,14},{9,15},{10,... | collective-permute-start | bytes 196616 | tf_op jit(solution)/shard_map/ppermute | solution.py:293

commit v4 on v3

--- a/solution.py
+++ b/solution.py
@@ -71,6 +71,11 @@
     out_ref[:, half:] = jnp.dot(high, recv, preferred_element_type=F32).astype(BF)
 
 
+def step(j, device):
+    core = device & 1
+    return device ^ (0, 2 + 2 * core, 4 + 2 * core, 6 - 4 * core)[j]
+
+
 def rotate(x, cos, sin):
     return x * cos + pltpu.roll(x, HD // 2, 1) * sin
 
@@ -89,7 +94,7 @@
     inv_rms = lax.rsqrt(total / D + EPS)
     for j in range(n_x):
         for c, ref in enumerate((mine_ref, other_ref)):
-            owner = (me ^ (2 * j)) ^ c
+            owner = step(j, me ^ c)
             cols = pl.ds(pl.multiple_of(owner * width, width), width)
             gain = gain_ref[:, cols].astype(F32)
             normed[:, cols] = (ref[j].astype(F32) * inv_rms * gain).astype(BF)
@@ -124,7 +129,7 @@
     ctx = jnp.concatenate([ctx[h * nodes : (h + 1) * nodes] for h in range(heads)], axis=1)
     ctx_ref[...] = ctx
     for j in range(n_x):
-        cols = pl.ds(pl.multiple_of(((me ^ (2 * j)) ^ 1) * width, width), width)
+        cols = pl.ds(pl.multiple_of(step(j, me ^ 1) * width, width), width)
         send_ref[j] = jnp.dot(ctx, wout_ref[:, cols], preferred_element_type=F32).astype(BF)
 
 
@@ -161,7 +166,7 @@
     n_x, _, width = out_ref.shape
     ctx = ctx_ref[...]
     for j in range(n_x):
-        cols = pl.ds(pl.multiple_of((idx_ref[0] ^ (2 * j)) * width, width), width)
+        cols = pl.ds(pl.multiple_of(step(j, idx_ref[0]) * width, width), width)
         out_ref[j] = jnp.dot(ctx, wout_ref[:, cols], preferred_element_type=F32)
 
 
@@ -242,7 +247,7 @@
         out_shape=jax.ShapeDtypeStruct((n_x, nodes, width), BF),
         compiler_params=limit(4),
         name="stack",
-    )(emb, *[lax.ppermute(emb, "tensor", swap(n_tp, 2 * j)) for j in range(1, n_x)], w_query)
+    )(emb, *[lax.ppermute(emb, "tensor", [(i, step(j, i)) for i in range(n_tp)]) for j in range(1, n_x)], w_query)
     other = lax.ppermute(mine, "tensor", swap(n_tp, 1))
 
     depth = jnp.sum(ancestors[0], axis=1) - 1
@@ -290,7 +295,7 @@
         compiler_params=limit(4),
         name="pair",
     )(own, came)
-    parts = [lax.ppermute(pairs[j], "tensor", swap(n_tp, 2 * j)) for j in range(1, n_x)]
+    parts = [lax.ppermute(pairs[j], "tensor", [(i, step(j, i)) for i in range(n_tp)]) for j in range(1, n_x)]
     return pl.pallas_call(
         final_kernel,
         in_specs=[vmem] * (n_x + 1),

time: 62.5 us -> 62.1 us (level)
  starting transfers between devices: 28.5 us -> 27.2 us
  waiting for transfers between devices: 18.9 us -> 19.7 us
    ppermute x6, waiting for transfers between devices: 3.69 us -> 4.53 us  [the longest x3 4.04 us: shards(): lax.ppermute(pairs[j], 'tensor', [(i, step(j, i)) for i in range(n_tp)])]
    ppermute x6, starting transfers between devices: 7.29 us -> 6.55 us  [the longest x3 3.75 us: shards(): lax.ppermute(emb, 'tensor', [(i, step(j, i)) for i in range(n_tp)])]
where the time goes in v4:
time: 62.1 us; the launch traced here: 61.7 us
  starting transfers between devices  27.2 us (44%)
  waiting for transfers between devices  19.7 us (32%)
  Pallas kernels  13.6 us (22%)
  between operations  0.82 us (1%)
    all_to_all x1, starting transfers between devices, shards(): lax.all_to_all(copies, 'dp', split_axis=0, concat_axis=0, tiled=True)  12 us
    all_to_all x1, waiting for transfers between devices, shards(): lax.all_to_all(copies, 'dp', split_axis=0, concat_axis=0, tiled=True)  6.93 us
    pallas_call x3, Pallas kernels, load(): pl.pallas_call(functools.partial(load_kernel, len(arrays)), out_shape=tup...  6.72 us
    all_to_all x1, waiting for transfers between devices, shards(): lax.all_to_all(rows.reshape(n_dp, 2 * CAP, width // 2), 'dp', split_axis=...  6.68 us
    ppermute x1, starting transfers between devices, shards(): other = lax.ppermute(mine, 'tensor', swap(n_tp, 1))  4.28 us
    ppermute x3, waiting for transfers between devices, shards(): lax.ppermute(pairs[j], 'tensor', [(i, step(j, i)) for i in range(n_tp)])  4.04 us
    all_to_all x1, starting transfers between devices, shards(): lax.all_to_all(rows.reshape(n_dp, 2 * CAP, width // 2), 'dp', split_axis=...  3.85 us
    ppermute x3, starting transfers between devices, shards(): lax.ppermute(emb, 'tensor', [(i, step(j, i)) for i in range(n_tp)])  3.75 us
  transfers between devices with their start and end apart: 10, of which 7 were waited for; matrix products, arithmetic and copies ran while one was open for 1% of the time, Pallas kernels for 12%

profile of v4, /device:TPU:1, one launch (start us, length us, event | category | flops | bytes accessed | tf_op | source)
XLA Modules:
  0.0 61.7 jit_solution(17073553711336448321)
XLA Ops:
  0.0 0.0 copy-start.4
  0.0 0.0 copy-start.2
  0.0 0.0 copy-start.1
  0.0 0.0 copy-start
  0.0 1.3 %spread.1 = s32[32,64]{1,0:T(8,128)} custom-call(s32[1,64]{1,0:T(1,128)} %ids_ref.3), custom_call_target="tpu_custom_call" | custom-call | tf_op jit(solution)/shard_map/spread/pallas_call | solution.py:211
  1.3 12.0 %all-to-all-start = ((s32[32,1,64]{2,1,0:T(1,128)}), s32[32,1,64]{2,1,0:T(1,128)S(1)}, u32[]{:S(2)}, u32[]{:S(2)}) async-start(s32[32,1,64]{2,1,0:T(1,128)} %bitcast.18), calls=%async_computation | async-start | bytes 32768 | tf_op jit(solution)/shard_map/all_to_all | solution.py:219
  13.4 0.0 copy-start.3
  13.4 1.6 %load.3.table_ref = bf16[2048,512]{1,0:T(8,128)(2,1)S(1)} custom-call(bf16[2048,512]{1,0:T(8,128)(2,1)} %refs_0_.3), custom_call_target="tpu_custom_call" | custom-call | bytes 2097152 | tf_op jit(solution)/shard_map/load/pallas_call | solution.py:150
  15.0 6.9 %all-to-all-done = s32[32,1,64]{2,1,0:T(1,128)S(1)} async-done(((s32[32,1,64]{2,1,0:T(1,128)}), s32[32,1,64]{2,1,0:T(1,128)S(1)}, u32[]{:S(2)}, u32[]{:S(2)}) %all-to-all-start) | async-done | bytes 8224 | tf_op jit(solution)/shard_map/all_to_all | solution.py:219
  21.9 1.4 %rows.1.refs_3_ = bf16[16,2,8,256]{3,2,1,0:T(8,128)(2,1)} custom-call(s32[1]{0:T(128)} %bitcast.idx_ref, s32[32,64]{1,0:T(8,128)S(1)} %bitcast.17, bf16[2048,512]{1,0:T(8,128)(2,1)S(1)} %load.3.table_ref), custom_call_target="tpu_custom_call" | custom-call | tf_op jit(solution)/shard_map/rows/pallas_call | solution.py:221
  23.4 3.9 %all-to-all-start.1 = ((bf16[32,8,256]{2,1,0:T(8,128)(2,1)}), bf16[32,8,256]{2,1,0:T(8,128)(2,1)S(1)}, u32[]{:S(2)}, u32[]{:S(2)}) async-start(bf16[32,8,256]{2,1,0:T(8,128)(2,1)} %bitcast.4), calls=%async_computation.1 | async-start | bytes 262144 | tf_op jit(solution)/shard_map/all_to_all | solution.py:230
  27.9 0.0 copy-done.4
  27.9 0.0 copy-done.2
  27.9 0.1 reduce_sum.9
  28.0 0.0 copy-done.1
  28.1 0.0 copy-done
  28.1 1.6 %load.4 = (bf16[2,4096,128]{2,1,0:T(8,128)(2,1)S(1)}, bf16[1,1,1024,128]{3,2,1,0:T(8,128)(2,1)S(1)}, bf16[1,1,1024,128]{3,2,1,0:T(8,128)(2,1)S(1)}) custom-call(bf16[2,4096,128]{2,1,0:T(8,128)(2,1)} %refs_0_.4, bf16[1,1,1024,128]{3,2,1,0:T(8,128)(2,1)S(1)} %copy-done, bf16[1,1,1024,128]{3,2,1,0:T(8,128)(2,1)S(1)} %copy-done.1, ...), custom_call_target="tpu_custom_call" | custom-call | bytes 2621440 | tf_op jit(solution)/shard_map/load/pallas_call | solution.py:150
  29.7 6.7 %all-to-all-done.1 = bf16[32,8,256]{2,1,0:T(8,128)(2,1)S(1)} async-done(((bf16[32,8,256]{2,1,0:T(8,128)(2,1)}), bf16[32,8,256]{2,1,0:T(8,128)(2,1)S(1)}, u32[]{:S(2)}, u32[]{:S(2)}) %all-to-all-start.1) | async-done | bytes 131104 | tf_op jit(solution)/shard_map/all_to_all | solution.py:230
  36.4 0.0 copy-done.3
  36.4 0.4 pick.1.refs_2_.refs_0_.emb_ref
  36.7 1.3 %collective-permute-start.2 = (bf16[64,512]{1,0:T(8,128)(2,1)S(1)}, bf16[64,512]{1,0:T(8,128)(2,1)S(1)}, u32[]{:S(2)}, u32[]{:S(2)}) collective-permute-start(bf16[64,512]{1,0:T(8,128)(2,1)S(1)} %pick.1.refs_2_.refs_0_.emb_ref), channel_id=1, source_target_pairs={{0,6},{1,3},{2,4},{3,1},{4,2},{5,7},{6,0},{7,5},{8,14},{9,11},{10,... | collective-permute-start | bytes 196616 | tf_op jit(solution)/shard_map/ppermute | solution.py:250
  38.0 1.8 %collective-permute-start.1 = (bf16[64,512]{1,0:T(8,128)(2,1)S(1)}, bf16[64,512]{1,0:T(8,128)(2,1)S(1)}, u32[]{:S(2)}, u32[]{:S(2)}) collective-permute-start(bf16[64,512]{1,0:T(8,128)(2,1)S(1)} %pick.1.refs_2_.refs_0_.emb_ref), channel_id=1, source_target_pairs={{0,4},{1,7},{2,6},{3,5},{4,0},{5,3},{6,2},{7,1},{8,12},{9,15},{10,... | collective-permute-start | bytes 196616 | tf_op jit(solution)/shard_map/ppermute | solution.py:250
  39.9 0.6 %collective-permute-start = (bf16[64,512]{1,0:T(8,128)(2,1)S(1)}, bf16[64,512]{1,0:T(8,128)(2,1)S(1)}, u32[]{:S(2)}, u32[]{:S(2)}) collective-permute-start(bf16[64,512]{1,0:T(8,128)(2,1)S(1)} %pick.1.refs_2_.refs_0_.emb_ref), channel_id=1, source_target_pairs={{0,2},{1,5},{2,0},{3,7},{4,6},{5,1},{6,4},{7,3},{8,10},{9,13},{10,... | collective-permute-start | bytes 196616 | tf_op jit(solution)/shard_map/ppermute | solution.py:250
  40.5 3.5 %load.5 = (bf16[4096,512]{1,0:T(8,128)(2,1)S(1)}, bf16[512,4096]{1,0:T(8,128)(2,1)S(1)}) custom-call(bf16[4096,512]{1,0:T(8,128)(2,1)} %refs_0_.5, bf16[512,4096]{1,0:T(8,128)(2,1)} %refs_1_.3, bf16[64,512]{1,0:T(8,128)(2,1)S(1)} %pick.1.refs_2_.refs_0_.emb_ref), custom_call_target="tpu_custom_call" | custom-call | bytes 8388608 | tf_op jit(solution)/shard_map/load/pallas_call | solution.py:150
  44.0 0.0 collective-permute-done.2.refs_3_
  44.0 0.0 collective-permute-done.1.refs_2_
  44.0 0.5 collective-permute-done.refs_1_
  44.5 4.3 %collective-permute-start.3 = (bf16[4,64,512]{2,1,0:T(8,128)(2,1)S(1)}, bf16[4,64,512]{2,1,0:T(8,128)(2,1)S(1)}, u32[]{:S(2)}, u32[]{:S(2)}) collective-permute-start(bf16[4,64,512]{2,1,0:T(8,128)(2,1)S(1)} %stack.1.mine_ref), channel_id=1, source_target_pairs={{0,1},{1,0},{2,3},{3,2},{4,5},{5,4},{6,7},{7,6},{8,9},{9,8},{10,11... | collective-permute-start | bytes 786440 | tf_op jit(solution)/shard_map/ppermute | solution.py:251
  48.8 0.2 fusion
  49.0 0.1 pad_maximum_fusion
  49.1 0.9 %collective-permute-done.3.other_ref = bf16[4,64,512]{2,1,0:T(8,128)(2,1)S(1)} collective-permute-done((bf16[4,64,512]{2,1,0:T(8,128)(2,1)S(1)}, bf16[4,64,512]{2,1,0:T(8,128)(2,1)S(1)}, u32[]{:S(2)}, u32[]{:S(2)}) %collective-permute-start.3) | collective-permute-done | bytes 262176 | tf_op jit(solution)/shard_map/ppermute | solution.py:251
  50.0 2.5 %layer.1 = (bf16[64,512]{1,0:T(8,128)(2,1)S(1)}, bf16[4,64,512]{2,1,0:T(8,128)(2,1)S(1)}) custom-call(s32[1]{0:T(128)} %bitcast.6.idx_ref, s32[1]{0:T(128)} %copy.12.len_ref, bf16[4,64,512]{2,1,0:T(8,128)(2,1)S(1)} %stack.1.mine_ref, bf16[4,64,512]{2,1,0:T(8,128)(2,1)S(1)} %collective-permute-done.3.other_ref, bf16[1,4096]{1,0:T(2,128)(2,1)S(1)} %reshape.31.gain_ref, ...), custom_call_target="tpu_custom_call" | custom-call | tf_op jit(solution)/shard_map/layer/pallas_call | solution.py:263
  52.5 0.5 collective-permute-start.4
  53.0 0.5 project.1.own_ref
  53.5 0.7 %collective-permute-done.4.came_ref = bf16[4,64,512]{2,1,0:T(8,128)(2,1)S(1)} collective-permute-done((bf16[4,64,512]{2,1,0:T(8,128)(2,1)S(1)}, bf16[4,64,512]{2,1,0:T(8,128)(2,1)S(1)}, u32[]{:S(2)}, u32[]{:S(2)}) %collective-permute-start.4) | collective-permute-done | bytes 262176 | tf_op jit(solution)/shard_map/ppermute | solution.py:278
  54.2 1.9 %collective-permute-start.5 = (bf16[64,512]{1,0:T(8,128)(2,1)S(1)}, bf16[64,512]{1,0:T(8,128)(2,1)S(1)}, u32[]{:S(2)}, u32[]{:S(2)}) collective-permute-start(bf16[64,512]{1,0:T(8,128)(2,1)S(1)} %get-tuple-element.24), channel_id=1, source_target_pairs={{0,2},{1,5},{2,0},{3,7},{4,6},{5,1},{6,4},{7,3},{8,10},{9,13},{10,... | collective-permute-start | bytes 196616 | tf_op jit(solution)/shard_map/ppermute | solution.py:298
  56.1 0.9 %collective-permute-start.6 = (bf16[64,512]{1,0:T(8,128)(2,1)S(1)}, bf16[64,512]{1,0:T(8,128)(2,1)S(1)}, u32[]{:S(2)}, u32[]{:S(2)}) collective-permute-start(bf16[64,512]{1,0:T(8,128)(2,1)S(1)} %get-tuple-element.25), channel_id=1, source_target_pairs={{0,4},{1,7},{2,6},{3,5},{4,0},{5,3},{6,2},{7,1},{8,12},{9,15},{10,... | collective-permute-start | bytes 196616 | tf_op jit(solution)/shard_map/ppermute | solution.py:298
  57.0 0.0 collective-permute-start.7
  57.0 2.0 %collective-permute-done.5.refs_0_ = bf16[64,512]{1,0:T(8,128)(2,1)S(1)} collective-permute-done((bf16[64,512]{1,0:T(8,128)(2,1)S(1)}, bf16[64,512]{1,0:T(8,128)(2,1)S(1)}, u32[]{:S(2)}, u32[]{:S(2)}) %collective-permute-start.5) | collective-permute-done | bytes 65568 | tf_op jit(solution)/shard_map/ppermute | solution.py:298
  59.0 2.0 %collective-permute-done.6.refs_1_ = bf16[64,512]{1,0:T(8,128)(2,1)S(1)} collective-permute-done((bf16[64,512]{1,0:T(8,128)(2,1)S(1)}, bf16[64,512]{1,0:T(8,128)(2,1)S(1)}, u32[]{:S(2)}, u32[]{:S(2)}) %collective-permute-start.6) | collective-permute-done | bytes 65568 | tf_op jit(solution)/shard_map/ppermute | solution.py:298
  61.0 0.0 collective-permute-done.7.refs_2_
  61.0 0.7 %final.1 = bf16[64,512]{1,0:T(8,128)(2,1)} custom-call(bf16[64,512]{1,0:T(8,128)(2,1)S(1)} %pick.1.refs_2_.refs_0_.emb_ref, f32[64,512]{1,0:T(8,128)S(1)} %get-tuple-element.23.own_ref, bf16[64,512]{1,0:T(8,128)(2,1)S(1)} %collective-permute-done.5.refs_0_, bf16[64,512]{1,0:T(8,128)(2,1)S(1)} %collective-permute-done.6.refs_1_, ...), custom_call_target="tpu_custom_call" | custom-call | tf_op jit(solution)/shard_map/final/pallas_call | solution.py:299
  (5 shorter events, 0.1 us)
Async XLA Ops:
  0.0 27.9 %copy-start.4 = (bf16[4096]{0:T(1024)(128)(2,1)S(1)}, bf16[4096]{0:T(1024)(128)(2,1)}, u32[]{:S(2)}) copy-start(bf16[4096]{0:T(1024)(128)(2,1)} %param.14) | copy-start | bytes 24580
  0.0 27.9 %copy-start.2 = (s32[1,64,64]{2,1,0:T(8,128)S(1)}, s32[1,64,64]{2,1,0:T(8,128)}, u32[]{:S(2)}) copy-start(s32[1,64,64]{2,1,0:T(8,128)} %param.11) | copy-start | bytes 49156
  0.0 28.0 %copy-start.1 = (bf16[1,1,1024,128]{3,2,1,0:T(8,128)(2,1)S(1)}, bf16[1,1,1024,128]{3,2,1,0:T(8,128)(2,1)}, u32[]{:S(2)}) copy-start(bf16[1,1,1024,128]{3,2,1,0:T(8,128)(2,1)} %refs_2_.1) | copy-start | bytes 786436
  0.0 28.0 %copy-start = (bf16[1,1,1024,128]{3,2,1,0:T(8,128)(2,1)S(1)}, bf16[1,1,1024,128]{3,2,1,0:T(8,128)(2,1)}, u32[]{:S(2)}) copy-start(bf16[1,1,1024,128]{3,2,1,0:T(8,128)(2,1)} %refs_1_.2) | copy-start | bytes 786436
  1.3 20.6 %all-to-all-start = ((s32[32,1,64]{2,1,0:T(1,128)}), s32[32,1,64]{2,1,0:T(1,128)S(1)}, u32[]{:S(2)}, u32[]{:S(2)}) async-start(s32[32,1,64]{2,1,0:T(1,128)} %bitcast.18), calls=%async_computation | async-start | bytes 32768 | tf_op jit(solution)/shard_map/all_to_all | solution.py:219
  13.4 23.0 %copy-start.3 = (s32[1,64]{1,0:T(1,128)S(1)}, s32[1,64]{1,0:T(1,128)}, u32[]{:S(2)}) copy-start(s32[1,64]{1,0:T(1,128)} %ids_ref.3) | copy-start | bytes 772
  23.4 13.0 %all-to-all-start.1 = ((bf16[32,8,256]{2,1,0:T(8,128)(2,1)}), bf16[32,8,256]{2,1,0:T(8,128)(2,1)S(1)}, u32[]{:S(2)}, u32[]{:S(2)}) async-start(bf16[32,8,256]{2,1,0:T(8,128)(2,1)} %bitcast.4), calls=%async_computation.1 | async-start | bytes 262144 | tf_op jit(solution)/shard_map/all_to_all | solution.py:230
  36.7 7.3 %collective-permute-start.2 = (bf16[64,512]{1,0:T(8,128)(2,1)S(1)}, bf16[64,512]{1,0:T(8,128)(2,1)S(1)}, u32[]{:S(2)}, u32[]{:S(2)}) collective-permute-start(bf16[64,512]{1,0:T(8,128)(2,1)S(1)} %pick.1.refs_2_.refs_0_.emb_ref), channel_id=1, source_target_pairs={{0,6},{1,3},{2,4},{3,1},{4,2},{5,7},{6,0},{7,5},{8,14},{9,11},{10,... | collective-permute-start | bytes 196616 | tf_op jit(solution)/shard_map/ppermute | solution.py:250
  38.0 6.0 %collective-permute-start.1 = (bf16[64,512]{1,0:T(8,128)(2,1)S(1)}, bf16[64,512]{1,0:T(8,128)(2,1)S(1)}, u32[]{:S(2)}, u32[]{:S(2)}) collective-permute-start(bf16[64,512]{1,0:T(8,128)(2,1)S(1)} %pick.1.refs_2_.refs_0_.emb_ref), channel_id=1, source_target_pairs={{0,4},{1,7},{2,6},{3,5},{4,0},{5,3},{6,2},{7,1},{8,12},{9,15},{10,... | collective-permute-start | bytes 196616 | tf_op jit(solution)/shard_map/ppermute | solution.py:250
  39.9 4.6 %collective-permute-start = (bf16[64,512]{1,0:T(8,128)(2,1)S(1)}, bf16[64,512]{1,0:T(8,128)(2,1)S(1)}, u32[]{:S(2)}, u32[]{:S(2)}) collective-permute-start(bf16[64,512]{1,0:T(8,128)(2,1)S(1)} %pick.1.refs_2_.refs_0_.emb_ref), channel_id=1, source_target_pairs={{0,2},{1,5},{2,0},{3,7},{4,6},{5,1},{6,4},{7,3},{8,10},{9,13},{10,... | collective-permute-start | bytes 196616 | tf_op jit(solution)/shard_map/ppermute | solution.py:250
  44.5 5.4 %collective-permute-start.3 = (bf16[4,64,512]{2,1,0:T(8,128)(2,1)S(1)}, bf16[4,64,512]{2,1,0:T(8,128)(2,1)S(1)}, u32[]{:S(2)}, u32[]{:S(2)}) collective-permute-start(bf16[4,64,512]{2,1,0:T(8,128)(2,1)S(1)} %stack.1.mine_ref), channel_id=1, source_target_pairs={{0,1},{1,0},{2,3},{3,2},{4,5},{5,4},{6,7},{7,6},{8,9},{9,8},{10,11... | collective-permute-start | bytes 786440 | tf_op jit(solution)/shard_map/ppermute | solution.py:251
  52.5 1.6 %collective-permute-start.4 = (bf16[4,64,512]{2,1,0:T(8,128)(2,1)S(1)}, bf16[4,64,512]{2,1,0:T(8,128)(2,1)S(1)}, u32[]{:S(2)}, u32[]{:S(2)}) collective-permute-start(bf16[4,64,512]{2,1,0:T(8,128)(2,1)S(1)} %get-tuple-element.22), channel_id=1, source_target_pairs={{0,1},{1,0},{2,3},{3,2},{4,5},{5,4},{6,7},{7,6},{8,9},{9,8},{10,11... | collective-permute-start | bytes 786440 | tf_op jit(solution)/shard_map/ppermute | solution.py:278
  54.2 4.8 %collective-permute-start.5 = (bf16[64,512]{1,0:T(8,128)(2,1)S(1)}, bf16[64,512]{1,0:T(8,128)(2,1)S(1)}, u32[]{:S(2)}, u32[]{:S(2)}) collective-permute-start(bf16[64,512]{1,0:T(8,128)(2,1)S(1)} %get-tuple-element.24), channel_id=1, source_target_pairs={{0,2},{1,5},{2,0},{3,7},{4,6},{5,1},{6,4},{7,3},{8,10},{9,13},{10,... | collective-permute-start | bytes 196616 | tf_op jit(solution)/shard_map/ppermute | solution.py:298
  56.1 4.9 %collective-permute-start.6 = (bf16[64,512]{1,0:T(8,128)(2,1)S(1)}, bf16[64,512]{1,0:T(8,128)(2,1)S(1)}, u32[]{:S(2)}, u32[]{:S(2)}) collective-permute-start(bf16[64,512]{1,0:T(8,128)(2,1)S(1)} %get-tuple-element.25), channel_id=1, source_target_pairs={{0,4},{1,7},{2,6},{3,5},{4,0},{5,3},{6,2},{7,1},{8,12},{9,15},{10,... | collective-permute-start | bytes 196616 | tf_op jit(solution)/shard_map/ppermute | solution.py:298
  57.0 4.0 %collective-permute-start.7 = (bf16[64,512]{1,0:T(8,128)(2,1)S(1)}, bf16[64,512]{1,0:T(8,128)(2,1)S(1)}, u32[]{:S(2)}, u32[]{:S(2)}) collective-permute-start(bf16[64,512]{1,0:T(8,128)(2,1)S(1)} %get-tuple-element.26), channel_id=1, source_target_pairs={{0,6},{1,3},{2,4},{3,1},{4,2},{5,7},{6,0},{7,5},{8,14},{9,11},{10,... | collective-permute-start | bytes 196616 | tf_op jit(solution)/shard_map/ppermute | solution.py:298

commit v5 on v4

--- a/solution.py
+++ b/solution.py
@@ -22,7 +22,7 @@
     return lax.broadcasted_iota(jnp.int32, shape, dim)
 
 
-def rows_kernel(idx_ref, ids_ref, table_ref, out_ref):
+def rows_kernel(idx_ref, ids_ref, table_ref, _, out_ref):
     vocab = table_ref.shape[0]
     n_dst, nodes = ids_ref.shape
     off = ids_ref[...] - idx_ref[0] * vocab
@@ -54,7 +54,7 @@
     out_ref[:, 1] = jnp.where(first, pltpu.roll(low_half, CAP, 1), high_half).astype(BF)
 
 
-def pick_kernel(ids_ref, recv_ref, _, out_ref, *, vocab):
+def pick_kernel(ids_ref, recv_ref, out_ref, *, vocab):
     nodes = ids_ref.shape[1]
     n_in, half = recv_ref.shape
     ids_row = jnp.broadcast_to(ids_ref[...], (nodes, nodes)) // vocab
@@ -76,15 +76,24 @@
     return device ^ (0, 2 + 2 * core, 4 + 2 * core, 6 - 4 * core)[j]
 
 
+def live_kernel(len_ref, out_ref):
+    out_ref[...] = jnp.full(out_ref.shape, len_ref[0], jnp.int32)
+
+
+def place_kernel(len_ref, anc_ref, _, out_ref):
+    depth = jnp.sum(anc_ref[...].astype(F32), axis=1, keepdims=True).astype(jnp.int32) - 1
+    out_ref[...] = jnp.broadcast_to((len_ref[:, 0:1] + depth).astype(F32), out_ref.shape)
+
+
 def rotate(x, cos, sin):
     return x * cos + pltpu.roll(x, HD // 2, 1) * sin
 
 
 def layer_kernel(
-    idx_ref, len_ref, mine_ref, other_ref, gain_ref, wq_ref, wkv_ref, wout_ref, kc_ref, vc_ref,
+    len_ref, mine_ref, other_ref, gain_ref, wq_ref, wkv_ref, wout_ref, kc_ref, vc_ref,
     anc_ref, cos_ref, sin_ref, ctx_ref, send_ref, normed,
 ):
-    me = idx_ref[0]
+    me = lax.axis_index("tensor")
     n_x, nodes, width = mine_ref.shape
     total = jnp.zeros((nodes, 1), F32)
     for j in range(n_x):
@@ -113,7 +122,7 @@
     scale = HD ** (-0.5)
     slots = kc_ref.shape[0]
     s_cache = lax.dot_general(group, kc_ref[...], contract, preferred_element_type=F32) * scale
-    s_cache = jnp.where(iota((1, slots), 1) < len_ref[0], s_cache, NEG)
+    s_cache = jnp.where(iota((1, slots), 1) < len_ref[:, 0:1], s_cache, NEG)
     s_tree = lax.dot_general(group, keys, contract, preferred_element_type=F32) * scale
     mask = jnp.concatenate([anc_ref[...]] * heads, axis=0)
     s_tree = jnp.where(mask > 0, s_tree, NEG)
@@ -162,11 +171,11 @@
     )(*arrays, *after)
 
 
-def out_kernel(idx_ref, ctx_ref, wout_ref, out_ref):
+def out_kernel(ctx_ref, wout_ref, out_ref):
     n_x, _, width = out_ref.shape
     ctx = ctx_ref[...]
     for j in range(n_x):
-        cols = pl.ds(pl.multiple_of(step(j, idx_ref[0]) * width, width), width)
+        cols = pl.ds(pl.multiple_of(step(j, lax.axis_index("tensor")) * width, width), width)
         out_ref[j] = jnp.dot(ctx, wout_ref[:, cols], preferred_element_type=F32)
 
 
@@ -202,8 +211,6 @@
     n_x = n_tp // 2
     nodes = tree_ids.shape[1]
     vocab, width = table.shape
-    me = lax.axis_index("tensor")
-    me_arr = me.astype(jnp.int32).reshape(1)
     part = lax.axis_index("dp").astype(jnp.int32).reshape(1)
     vmem = pl.BlockSpec(memory_space=pltpu.VMEM)
     smem = pl.BlockSpec(memory_space=pltpu.SMEM)
@@ -217,28 +224,36 @@
         name="spread",
     )(tree_ids)
     all_ids = lax.all_to_all(copies, "dp", split_axis=0, concat_axis=0, tiled=True)
+    live = pl.pallas_call(
+        live_kernel,
+        out_shape=jax.ShapeDtypeStruct((1, HD), jnp.int32),
+        in_specs=[smem],
+        out_specs=vmem,
+        compiler_params=limit(4),
+        name="live",
+    )(lengths)
     (table_held,) = load((table,), (), 50)
     rows = pl.pallas_call(
         rows_kernel,
         out_shape=jax.ShapeDtypeStruct((n_dp // 2, 2, 2 * CAP, width // 2), BF),
-        in_specs=[smem, vmem, vmem],
+        in_specs=[smem, vmem, vmem, pl.BlockSpec(memory_space=pl.ANY)],
         out_specs=vmem,
         compiler_params=limit(12),
         name="rows",
-    )(part, all_ids, table_held)
-    w_kv, key_cache, value_cache = load((w_kv, key_cache, value_cache), (rows,), 50)
+    )(part, all_ids, table_held, live)
     recv = lax.all_to_all(
         rows.reshape(n_dp, 2 * CAP, width // 2), "dp", split_axis=0, concat_axis=0, tiled=True
     )
     emb = pl.pallas_call(
         functools.partial(pick_kernel, vocab=vocab),
         out_shape=jax.ShapeDtypeStruct((nodes, width), BF),
-        in_specs=[vmem, vmem, pl.BlockSpec(memory_space=pl.ANY)],
+        in_specs=[vmem, vmem],
         out_specs=vmem,
         compiler_params=limit(4),
         name="pick",
-    )(tree_ids, recv.reshape(n_dp * 2 * CAP, width // 2), w_kv)
-
+    )(tree_ids, recv.reshape(n_dp * 2 * CAP, width // 2))
+
+    gain, emb = lax.optimization_barrier((gain, emb))
     w_query, w_out = load((w_query, w_out), (emb,), 45)
     mine = pl.pallas_call(
         stack_kernel,
@@ -250,11 +265,17 @@
     )(emb, *[lax.ppermute(emb, "tensor", [(i, step(j, i)) for i in range(n_tp)]) for j in range(1, n_x)], w_query)
     other = lax.ppermute(mine, "tensor", swap(n_tp, 1))
 
-    depth = jnp.sum(ancestors[0], axis=1) - 1
-    positions = (lengths[0] + depth).astype(F32)
+    positions = pl.pallas_call(
+        place_kernel,
+        out_shape=jax.ShapeDtypeStruct((nodes, HD // 2), F32),
+        in_specs=[vmem, vmem, pl.BlockSpec(memory_space=pl.ANY)],
+        out_specs=vmem,
+        compiler_params=limit(4),
+        name="place",
+    )(live, ancestors[0], emb)
     freq_index = jnp.arange(HD // 2, dtype=F32)
     inverse = jnp.exp(freq_index * (-2.0 * math.log(THETA) / HD))
-    angles = positions[:, None] * inverse[None, :]
+    angles = positions * inverse[None, :]
     cosine = jnp.cos(angles)
     sine = jnp.sin(angles)
     cos = jnp.concatenate([cosine, cosine], axis=1)
@@ -266,19 +287,19 @@
             jax.ShapeDtypeStruct((nodes, width), BF),
             jax.ShapeDtypeStruct((n_x, nodes, width), BF),
         ),
-        in_specs=[smem, smem] + [vmem] * 11,
+        in_specs=[vmem] * 12,
         out_specs=(vmem, vmem),
         scratch_shapes=[pltpu.VMEM((nodes, n_tp * width), BF)],
         compiler_params=limit(16),
         name="layer",
     )(
-        me_arr, lengths, mine, other, gain.reshape(1, -1), w_query, w_kv, w_out,
+        live, mine, other, gain.reshape(1, -1), w_query, w_kv, w_out,
         key_cache[0, 0], value_cache[0, 0], ancestors[0], cos, sin,
     )
     came = lax.ppermute(send, "tensor", swap(n_tp, 1))
     own = pl.pallas_call(
         out_kernel,
-        in_specs=[smem, vmem, vmem],
+        in_specs=[vmem, vmem],
         out_specs=vmem,
         out_shape=jax.ShapeDtypeStruct((n_x, nodes, width), F32),
         cost_estimate=pl.CostEstimate(
@@ -286,7 +307,7 @@
         ),
         compiler_params=limit(8),
         name="project",
-    )(me_arr, ctx, w_out)
+    )(ctx, w_out)
     pairs = pl.pallas_call(
         pair_kernel,
         in_specs=[vmem, vmem],

time: 62.1 us -> 60.8 us (0.979)
  blocking collectives: 0 us -> 12.1 us
  waiting for transfers between devices: 19.7 us -> 12.2 us
  starting transfers between devices: 27.2 us -> 23.6 us
  Pallas kernels: 13.6 us -> 11.5 us
    all_to_all x0 -> x1, blocking collectives: none -> 12.1 us  [shards(): lax.all_to_all(rows.reshape(n_dp, 2 * CAP, width // 2), 'dp', split_axis=...]
    all_to_all x1 -> x0, waiting for transfers between devices: 6.68 us -> none  [shards(): lax.all_to_all(rows.reshape(n_dp, 2 * CAP, width // 2), 'dp', split_axis=...]
    all_to_all x1 -> x0, starting transfers between devices: 3.85 us -> none  [shards(): lax.all_to_all(rows.reshape(n_dp, 2 * CAP, width // 2), 'dp', split_axis=...]
    pallas_call x3 -> x2, Pallas kernels: 6.72 us -> 5.1 us  [load(): pl.pallas_call(functools.partial(load_kernel, len(arrays)), out_shape=tup...]
    pallas_call x1, Pallas kernels: 1.43 us -> 0.78 us  [shards(): pl.pallas_call(rows_kernel, out_shape=jax.ShapeDtypeStruct((n_dp // 2, 2,...]
    all_to_all x1, waiting for transfers between devices: 6.93 us -> 6.29 us  [shards(): lax.all_to_all(copies, 'dp', split_axis=0, concat_axis=0, tiled=True)]
  transfers between devices with their start and end apart: 10 -> 9, of which waited for: 7 -> 6; matrix products, arithmetic and copies ran while one was open for 1% -> 0% of each run, Pallas kernels for 12% -> 10%
where the time goes in v5:
time: 60.8 us; the launch traced here: 60.4 us
  starting transfers between devices  23.6 us (39%)
  waiting for transfers between devices  12.2 us (20%)
  blocking collectives  12.1 us (20%)
  Pallas kernels  11.5 us (19%)
  between operations  0.79 us (1%)
    all_to_all x1, blocking collectives, shards(): lax.all_to_all(rows.reshape(n_dp, 2 * CAP, width // 2), 'dp', split_axis=...  12.1 us
    all_to_all x1, starting transfers between devices, shards(): lax.all_to_all(copies, 'dp', split_axis=0, concat_axis=0, tiled=True)  12 us
    all_to_all x1, waiting for transfers between devices, shards(): lax.all_to_all(copies, 'dp', split_axis=0, concat_axis=0, tiled=True)  6.29 us
    pallas_call x2, Pallas kernels, load(): pl.pallas_call(functools.partial(load_kernel, len(arrays)), out_shape=tup...  5.1 us
    ppermute x1, starting transfers between devices, shards(): other = lax.ppermute(mine, 'tensor', swap(n_tp, 1))  4.28 us
    ppermute x3, waiting for transfers between devices, shards(): lax.ppermute(pairs[j], 'tensor', [(i, step(j, i)) for i in range(n_tp)])  4.04 us
    ppermute x3, starting transfers between devices, shards(): lax.ppermute(emb, 'tensor', [(i, step(j, i)) for i in range(n_tp)])  3.75 us
    ppermute x3, starting transfers between devices, shards(): lax.ppermute(pairs[j], 'tensor', [(i, step(j, i)) for i in range(n_tp)])  3.04 us
  transfers between devices with their start and end apart: 9, of which 6 were waited for; matrix products, arithmetic and copies ran while one was open for 0% of the time, Pallas kernels for 10%

profile of v5, /device:TPU:1, one launch (start us, length us, event | category | flops | bytes accessed | tf_op | source)
XLA Modules:
  0.0 60.4 jit_solution(1371970126002268599)
XLA Ops:
  0.0 0.0 copy-start.4
  0.0 0.0 copy-start.5
  0.0 0.0 copy-start.3
  0.0 1.3 %spread.1 = s32[32,64]{1,0:T(8,128)} custom-call(s32[1,64]{1,0:T(1,128)} %ids_ref.3), custom_call_target="tpu_custom_call" | custom-call | tf_op jit(solution)/shard_map/spread/pallas_call | solution.py:218
  1.3 12.0 %all-to-all-start = ((s32[32,1,64]{2,1,0:T(1,128)}), s32[32,1,64]{2,1,0:T(1,128)S(1)}, u32[]{:S(2)}, u32[]{:S(2)}) async-start(s32[32,1,64]{2,1,0:T(1,128)} %bitcast.17), calls=%async_computation | async-start | bytes 32768 | tf_op jit(solution)/shard_map/all_to_all | solution.py:226
  14.0 1.6 %load.2.table_ref = bf16[2048,512]{1,0:T(8,128)(2,1)S(1)} custom-call(bf16[2048,512]{1,0:T(8,128)(2,1)} %refs_0_.2), custom_call_target="tpu_custom_call" | custom-call | bytes 2097152 | tf_op jit(solution)/shard_map/load/pallas_call | solution.py:159
  15.7 6.3 %all-to-all-done = s32[32,1,64]{2,1,0:T(1,128)S(1)} async-done(((s32[32,1,64]{2,1,0:T(1,128)}), s32[32,1,64]{2,1,0:T(1,128)S(1)}, u32[]{:S(2)}, u32[]{:S(2)}) %all-to-all-start) | async-done | bytes 8224 | tf_op jit(solution)/shard_map/all_to_all | solution.py:226
  21.9 0.8 %rows.1 = bf16[16,2,8,256]{3,2,1,0:T(8,128)(2,1)S(1)} custom-call(s32[1]{0:T(128)} %bitcast.idx_ref, s32[32,64]{1,0:T(8,128)S(1)} %bitcast.16, bf16[2048,512]{1,0:T(8,128)(2,1)S(1)} %load.2.table_ref, s32[1,128]{1,0:T(1,128)S(1)} %live.1._.len_ref), custom_call_target="tpu_custom_call" | custom-call | tf_op jit(solution)/shard_map/rows/pallas_call | solution.py:236
  22.7 12.1 %all_to_all.16 = bf16[32,8,256]{2,1,0:T(8,128)(2,1)S(1)} all-to-all(bf16[32,8,256]{2,1,0:T(8,128)(2,1)S(1)} %bitcast.10), channel_id=1, replica_groups=mesh['dp'=32,'tensor'=8] {'dp'}, dimensions={0} | all-to-all | bytes 262144 | tf_op jit(solution)/shard_map/all_to_all | solution.py:244
  34.8 0.0 copy-done.4
  34.8 0.4 pick.1.refs_2_.refs_0_._.emb_ref
  35.2 1.3 %collective-permute-start.2 = (bf16[64,512]{1,0:T(8,128)(2,1)S(1)}, bf16[64,512]{1,0:T(8,128)(2,1)S(1)}, u32[]{:S(2)}, u32[]{:S(2)}) collective-permute-start(bf16[64,512]{1,0:T(8,128)(2,1)S(1)} %pick.1.refs_2_.refs_0_._.emb_ref), channel_id=1, source_target_pairs={{0,6},{1,3},{2,4},{3,1},{4,2},{5,7},{6,0},{7,5},{8,14},{9,11},{10,... | collective-permute-start | bytes 196616 | tf_op jit(solution)/shard_map/ppermute | solution.py:265
  36.5 1.8 %collective-permute-start.1 = (bf16[64,512]{1,0:T(8,128)(2,1)S(1)}, bf16[64,512]{1,0:T(8,128)(2,1)S(1)}, u32[]{:S(2)}, u32[]{:S(2)}) collective-permute-start(bf16[64,512]{1,0:T(8,128)(2,1)S(1)} %pick.1.refs_2_.refs_0_._.emb_ref), channel_id=1, source_target_pairs={{0,4},{1,7},{2,6},{3,5},{4,0},{5,3},{6,2},{7,1},{8,12},{9,15},{10,... | collective-permute-start | bytes 196616 | tf_op jit(solution)/shard_map/ppermute | solution.py:265
  38.3 0.6 %collective-permute-start = (bf16[64,512]{1,0:T(8,128)(2,1)S(1)}, bf16[64,512]{1,0:T(8,128)(2,1)S(1)}, u32[]{:S(2)}, u32[]{:S(2)}) collective-permute-start(bf16[64,512]{1,0:T(8,128)(2,1)S(1)} %pick.1.refs_2_.refs_0_._.emb_ref), channel_id=1, source_target_pairs={{0,2},{1,5},{2,0},{3,7},{4,6},{5,1},{6,4},{7,3},{8,10},{9,13},{10,... | collective-permute-start | bytes 196616 | tf_op jit(solution)/shard_map/ppermute | solution.py:265
  39.0 0.0 copy-done.5
  39.0 0.0 copy-done.3
  39.0 0.2 place.1
  39.2 3.5 %load.3 = (bf16[4096,512]{1,0:T(8,128)(2,1)S(1)}, bf16[512,4096]{1,0:T(8,128)(2,1)S(1)}) custom-call(bf16[4096,512]{1,0:T(8,128)(2,1)} %refs_0_.3, bf16[512,4096]{1,0:T(8,128)(2,1)} %refs_1_.1, bf16[64,512]{1,0:T(8,128)(2,1)S(1)} %pick.1.refs_2_.refs_0_._.emb_ref), custom_call_target="tpu_custom_call" | custom-call | bytes 8388608 | tf_op jit(solution)/shard_map/load/pallas_call | solution.py:159
  42.7 0.0 copy-start
  42.7 0.0 copy-start.1
  42.7 0.0 copy-start.2
  42.7 0.0 collective-permute-done.2.refs_3_
  42.7 0.0 collective-permute-done.1.refs_2_
  42.7 0.2 collective-permute-done.refs_1_
  43.0 4.3 %collective-permute-start.3 = (bf16[4,64,512]{2,1,0:T(8,128)(2,1)S(1)}, bf16[4,64,512]{2,1,0:T(8,128)(2,1)S(1)}, u32[]{:S(2)}, u32[]{:S(2)}) collective-permute-start(bf16[4,64,512]{2,1,0:T(8,128)(2,1)S(1)} %stack.1.mine_ref), channel_id=1, source_target_pairs={{0,1},{1,0},{2,3},{3,2},{4,5},{5,4},{6,7},{7,6},{8,9},{9,8},{10,11... | collective-permute-start | bytes 786440 | tf_op jit(solution)/shard_map/ppermute | solution.py:266
  47.3 0.1 fusion
  47.4 0.1 pad_maximum_fusion
  47.5 0.9 %collective-permute-done.3.other_ref = bf16[4,64,512]{2,1,0:T(8,128)(2,1)S(1)} collective-permute-done((bf16[4,64,512]{2,1,0:T(8,128)(2,1)S(1)}, bf16[4,64,512]{2,1,0:T(8,128)(2,1)S(1)}, u32[]{:S(2)}, u32[]{:S(2)}) %collective-permute-start.3) | collective-permute-done | bytes 262176 | tf_op jit(solution)/shard_map/ppermute | solution.py:266
  48.4 0.0 copy-done
  48.4 0.0 copy-done.1
  48.4 0.0 copy-done.2
  48.4 2.5 %layer.1 = (bf16[64,512]{1,0:T(8,128)(2,1)S(1)}, bf16[4,64,512]{2,1,0:T(8,128)(2,1)S(1)}) custom-call(s32[1,128]{1,0:T(1,128)S(1)} %live.1._.len_ref, bf16[4,64,512]{2,1,0:T(8,128)(2,1)S(1)} %stack.1.mine_ref, bf16[4,64,512]{2,1,0:T(8,128)(2,1)S(1)} %collective-permute-done.3.other_ref, bf16[1,4096]{1,0:T(2,128)(2,1)S(1)} %reshape.22.gain_ref, ...), custom_call_target="tpu_custom_call" | custom-call | tf_op jit(solution)/shard_map/layer/pallas_call | solution.py:284
  51.0 0.5 collective-permute-start.4
  51.5 0.5 project.1.own_ref
  52.0 0.7 %collective-permute-done.4.came_ref = bf16[4,64,512]{2,1,0:T(8,128)(2,1)S(1)} collective-permute-done((bf16[4,64,512]{2,1,0:T(8,128)(2,1)S(1)}, bf16[4,64,512]{2,1,0:T(8,128)(2,1)S(1)}, u32[]{:S(2)}, u32[]{:S(2)}) %collective-permute-start.4) | collective-permute-done | bytes 262176 | tf_op jit(solution)/shard_map/ppermute | solution.py:299
  52.7 2.2 %collective-permute-start.5 = (bf16[64,512]{1,0:T(8,128)(2,1)S(1)}, bf16[64,512]{1,0:T(8,128)(2,1)S(1)}, u32[]{:S(2)}, u32[]{:S(2)}) collective-permute-start(bf16[64,512]{1,0:T(8,128)(2,1)S(1)} %get-tuple-element.22), channel_id=1, source_target_pairs={{0,2},{1,5},{2,0},{3,7},{4,6},{5,1},{6,4},{7,3},{8,10},{9,13},{10,... | collective-permute-start | bytes 196616 | tf_op jit(solution)/shard_map/ppermute | solution.py:319
  54.9 0.9 %collective-permute-start.6 = (bf16[64,512]{1,0:T(8,128)(2,1)S(1)}, bf16[64,512]{1,0:T(8,128)(2,1)S(1)}, u32[]{:S(2)}, u32[]{:S(2)}) collective-permute-start(bf16[64,512]{1,0:T(8,128)(2,1)S(1)} %get-tuple-element.23), channel_id=1, source_target_pairs={{0,4},{1,7},{2,6},{3,5},{4,0},{5,3},{6,2},{7,1},{8,12},{9,15},{10,... | collective-permute-start | bytes 196616 | tf_op jit(solution)/shard_map/ppermute | solution.py:319
  55.7 0.0 collective-permute-start.7
  55.7 1.7 %collective-permute-done.5.refs_0_ = bf16[64,512]{1,0:T(8,128)(2,1)S(1)} collective-permute-done((bf16[64,512]{1,0:T(8,128)(2,1)S(1)}, bf16[64,512]{1,0:T(8,128)(2,1)S(1)}, u32[]{:S(2)}, u32[]{:S(2)}) %collective-permute-start.5) | collective-permute-done | bytes 65568 | tf_op jit(solution)/shard_map/ppermute | solution.py:319
  57.4 2.4 %collective-permute-done.6.refs_1_ = bf16[64,512]{1,0:T(8,128)(2,1)S(1)} collective-permute-done((bf16[64,512]{1,0:T(8,128)(2,1)S(1)}, bf16[64,512]{1,0:T(8,128)(2,1)S(1)}, u32[]{:S(2)}, u32[]{:S(2)}) %collective-permute-start.6) | collective-permute-done | bytes 65568 | tf_op jit(solution)/shard_map/ppermute | solution.py:319
  59.8 0.0 collective-permute-done.7.refs_2_
  59.8 0.7 %final.1 = bf16[64,512]{1,0:T(8,128)(2,1)} custom-call(bf16[64,512]{1,0:T(8,128)(2,1)S(1)} %pick.1.refs_2_.refs_0_._.emb_ref, f32[64,512]{1,0:T(8,128)S(1)} %get-tuple-element.21.own_ref, bf16[64,512]{1,0:T(8,128)(2,1)S(1)} %collective-permute-done.5.refs_0_, bf16[64,512]{1,0:T(8,128)(2,1)S(1)} %collective-permute-done.6.refs_1_, ...), custom_call_target="tpu_custom_call" | custom-call | tf_op jit(solution)/shard_map/final/pallas_call | solution.py:320
  (5 shorter events, 0.1 us)
Async XLA Ops:
  0.0 34.8 %copy-start.4 = (s32[1,64]{1,0:T(1,128)S(1)}, s32[1,64]{1,0:T(1,128)}, u32[]{:S(2)}) copy-start(s32[1,64]{1,0:T(1,128)} %ids_ref.3) | copy-start | bytes 772
  0.0 39.0 %copy-start.5 = (bf16[4096]{0:T(1024)(128)(2,1)S(1)}, bf16[4096]{0:T(1024)(128)(2,1)}, u32[]{:S(2)}) copy-start(bf16[4096]{0:T(1024)(128)(2,1)} %param.14) | copy-start | bytes 24580
  0.0 39.0 %copy-start.3 = (s32[1,64,64]{2,1,0:T(8,128)S(1)}, s32[1,64,64]{2,1,0:T(8,128)}, u32[]{:S(2)}) copy-start(s32[1,64,64]{2,1,0:T(8,128)} %param.11) | copy-start | bytes 49156
  1.3 20.6 %all-to-all-start = ((s32[32,1,64]{2,1,0:T(1,128)}), s32[32,1,64]{2,1,0:T(1,128)S(1)}, u32[]{:S(2)}, u32[]{:S(2)}) async-start(s32[32,1,64]{2,1,0:T(1,128)} %bitcast.17), calls=%async_computation | async-start | bytes 32768 | tf_op jit(solution)/shard_map/all_to_all | solution.py:226
  35.2 7.5 %collective-permute-start.2 = (bf16[64,512]{1,0:T(8,128)(2,1)S(1)}, bf16[64,512]{1,0:T(8,128)(2,1)S(1)}, u32[]{:S(2)}, u32[]{:S(2)}) collective-permute-start(bf16[64,512]{1,0:T(8,128)(2,1)S(1)} %pick.1.refs_2_.refs_0_._.emb_ref), channel_id=1, source_target_pairs={{0,6},{1,3},{2,4},{3,1},{4,2},{5,7},{6,0},{7,5},{8,14},{9,11},{10,... | collective-permute-start | bytes 196616 | tf_op jit(solution)/shard_map/ppermute | solution.py:265
  36.5 6.2 %collective-permute-start.1 = (bf16[64,512]{1,0:T(8,128)(2,1)S(1)}, bf16[64,512]{1,0:T(8,128)(2,1)S(1)}, u32[]{:S(2)}, u32[]{:S(2)}) collective-permute-start(bf16[64,512]{1,0:T(8,128)(2,1)S(1)} %pick.1.refs_2_.refs_0_._.emb_ref), channel_id=1, source_target_pairs={{0,4},{1,7},{2,6},{3,5},{4,0},{5,3},{6,2},{7,1},{8,12},{9,15},{10,... | collective-permute-start | bytes 196616 | tf_op jit(solution)/shard_map/ppermute | solution.py:265
  38.3 4.6 %collective-permute-start = (bf16[64,512]{1,0:T(8,128)(2,1)S(1)}, bf16[64,512]{1,0:T(8,128)(2,1)S(1)}, u32[]{:S(2)}, u32[]{:S(2)}) collective-permute-start(bf16[64,512]{1,0:T(8,128)(2,1)S(1)} %pick.1.refs_2_.refs_0_._.emb_ref), channel_id=1, source_target_pairs={{0,2},{1,5},{2,0},{3,7},{4,6},{5,1},{6,4},{7,3},{8,10},{9,13},{10,... | collective-permute-start | bytes 196616 | tf_op jit(solution)/shard_map/ppermute | solution.py:265
  42.7 5.8 %copy-start = (bf16[2,4096,128]{2,1,0:T(8,128)(2,1)S(1)}, bf16[2,4096,128]{2,1,0:T(8,128)(2,1)}, u32[]{:S(2)}) copy-start(bf16[2,4096,128]{2,1,0:T(8,128)(2,1)} %wkv_ref.1) | copy-start | bytes 6291460
  42.7 5.7 %copy-start.1 = (bf16[1,1,1024,128]{3,2,1,0:T(8,128)(2,1)S(1)}, bf16[1,1,1024,128]{3,2,1,0:T(8,128)(2,1)}, u32[]{:S(2)}) copy-start(bf16[1,1,1024,128]{3,2,1,0:T(8,128)(2,1)} %param.18) | copy-start | bytes 786436
  42.7 5.7 %copy-start.2 = (bf16[1,1,1024,128]{3,2,1,0:T(8,128)(2,1)S(1)}, bf16[1,1,1024,128]{3,2,1,0:T(8,128)(2,1)}, u32[]{:S(2)}) copy-start(bf16[1,1,1024,128]{3,2,1,0:T(8,128)(2,1)} %param.19) | copy-start | bytes 786436
  43.0 5.4 %collective-permute-start.3 = (bf16[4,64,512]{2,1,0:T(8,128)(2,1)S(1)}, bf16[4,64,512]{2,1,0:T(8,128)(2,1)S(1)}, u32[]{:S(2)}, u32[]{:S(2)}) collective-permute-start(bf16[4,64,512]{2,1,0:T(8,128)(2,1)S(1)} %stack.1.mine_ref), channel_id=1, source_target_pairs={{0,1},{1,0},{2,3},{3,2},{4,5},{5,4},{6,7},{7,6},{8,9},{9,8},{10,11... | collective-permute-start | bytes 786440 | tf_op jit(solution)/shard_map/ppermute | solution.py:266
  51.0 1.6 %collective-permute-start.4 = (bf16[4,64,512]{2,1,0:T(8,128)(2,1)S(1)}, bf16[4,64,512]{2,1,0:T(8,128)(2,1)S(1)}, u32[]{:S(2)}, u32[]{:S(2)}) collective-permute-start(bf16[4,64,512]{2,1,0:T(8,128)(2,1)S(1)} %get-tuple-element.20), channel_id=1, source_target_pairs={{0,1},{1,0},{2,3},{3,2},{4,5},{5,4},{6,7},{7,6},{8,9},{9,8},{10,11... | collective-permute-start | bytes 786440 | tf_op jit(solution)/shard_map/ppermute | solution.py:299
  52.7 4.7 %collective-permute-start.5 = (bf16[64,512]{1,0:T(8,128)(2,1)S(1)}, bf16[64,512]{1,0:T(8,128)(2,1)S(1)}, u32[]{:S(2)}, u32[]{:S(2)}) collective-permute-start(bf16[64,512]{1,0:T(8,128)(2,1)S(1)} %get-tuple-element.22), channel_id=1, source_target_pairs={{0,2},{1,5},{2,0},{3,7},{4,6},{5,1},{6,4},{7,3},{8,10},{9,13},{10,... | collective-permute-start | bytes 196616 | tf_op jit(solution)/shard_map/ppermute | solution.py:319
  54.9 4.9 %collective-permute-start.6 = (bf16[64,512]{1,0:T(8,128)(2,1)S(1)}, bf16[64,512]{1,0:T(8,128)(2,1)S(1)}, u32[]{:S(2)}, u32[]{:S(2)}) collective-permute-start(bf16[64,512]{1,0:T(8,128)(2,1)S(1)} %get-tuple-element.23), channel_id=1, source_target_pairs={{0,4},{1,7},{2,6},{3,5},{4,0},{5,3},{6,2},{7,1},{8,12},{9,15},{10,... | collective-permute-start | bytes 196616 | tf_op jit(solution)/shard_map/ppermute | solution.py:319
  55.7 4.0 %collective-permute-start.7 = (bf16[64,512]{1,0:T(8,128)(2,1)S(1)}, bf16[64,512]{1,0:T(8,128)(2,1)S(1)}, u32[]{:S(2)}, u32[]{:S(2)}) collective-permute-start(bf16[64,512]{1,0:T(8,128)(2,1)S(1)} %get-tuple-element.24), channel_id=1, source_target_pairs={{0,6},{1,3},{2,4},{3,1},{4,2},{5,7},{6,0},{7,5},{8,14},{9,11},{10,... | collective-permute-start | bytes 196616 | tf_op jit(solution)/shard_map/ppermute | solution.py:319

commit v6 on v5

--- a/solution.py
+++ b/solution.py
@@ -73,7 +73,7 @@
 
 def step(j, device):
     core = device & 1
-    return device ^ (0, 2 + 2 * core, 4 + 2 * core, 6 - 4 * core)[j]
+    return device ^ (0, 2 + 4 * core, 4, 6 - 4 * core)[j]
 
 
 def live_kernel(len_ref, out_ref):

time: 60.8 us -> 60.8 us (level)
  waiting for transfers between devices: 12.2 us -> 13 us
  starting transfers between devices: 23.6 us -> 22.9 us
    ppermute x1, starting transfers between devices: 4.28 us -> 3.1 us  [shards(): other = lax.ppermute(mine, 'tensor', swap(n_tp, 1))]
    ppermute x3, waiting for transfers between devices: 0.23 us -> 1.22 us  [shards(): lax.ppermute(emb, 'tensor', [(i, step(j, i)) for i in range(n_tp)])]
  transfers between devices with their start and end apart: 9 -> 9, of which waited for: 6 -> 6; matrix products, arithmetic and copies ran while one was open for 0% -> 0% of each run, Pallas kernels for 10% -> 9%
where the time goes in v6:
time: 60.8 us; the launch traced here: 60.6 us
  starting transfers between devices  22.9 us (38%)
  waiting for transfers between devices  13 us (21%)
  blocking collectives  12.1 us (20%)
  Pallas kernels  11.5 us (19%)
  between operations  0.79 us (1%)
    all_to_all x1, blocking collectives, shards(): lax.all_to_all(rows.reshape(n_dp, 2 * CAP, width // 2), 'dp', split_axis=...  12.1 us
    all_to_all x1, starting transfers between devices, shards(): lax.all_to_all(copies, 'dp', split_axis=0, concat_axis=0, tiled=True)  12 us
    all_to_all x1, waiting for transfers between devices, shards(): lax.all_to_all(copies, 'dp', split_axis=0, concat_axis=0, tiled=True)  6.29 us
    pallas_call x2, Pallas kernels, load(): pl.pallas_call(functools.partial(load_kernel, len(arrays)), out_shape=tup...  5.1 us
    ppermute x3, starting transfers between devices, shards(): lax.ppermute(emb, 'tensor', [(i, step(j, i)) for i in range(n_tp)])  3.95 us
    ppermute x3, waiting for transfers between devices, shards(): lax.ppermute(pairs[j], 'tensor', [(i, step(j, i)) for i in range(n_tp)])  3.87 us
    ppermute x3, starting transfers between devices, shards(): lax.ppermute(pairs[j], 'tensor', [(i, step(j, i)) for i in range(n_tp)])  3.34 us
    ppermute x1, starting transfers between devices, shards(): other = lax.ppermute(mine, 'tensor', swap(n_tp, 1))  3.1 us
  transfers between devices with their start and end apart: 9, of which 6 were waited for; matrix products, arithmetic and copies ran while one was open for 0% of the time, Pallas kernels for 9%

profile of v6, /device:TPU:1, one launch (start us, length us, event | category | flops | bytes accessed | tf_op | source)
XLA Modules:
  0.0 60.6 jit_solution(8018454145346744162)
XLA Ops:
  0.0 0.0 copy-start.4
  0.0 0.0 copy-start.5
  0.0 0.0 copy-start.3
  0.0 1.3 %spread.1 = s32[32,64]{1,0:T(8,128)} custom-call(s32[1,64]{1,0:T(1,128)} %ids_ref.3), custom_call_target="tpu_custom_call" | custom-call | tf_op jit(solution)/shard_map/spread/pallas_call | solution.py:218
  1.3 12.0 %all-to-all-start = ((s32[32,1,64]{2,1,0:T(1,128)}), s32[32,1,64]{2,1,0:T(1,128)S(1)}, u32[]{:S(2)}, u32[]{:S(2)}) async-start(s32[32,1,64]{2,1,0:T(1,128)} %bitcast.17), calls=%async_computation | async-start | bytes 32768 | tf_op jit(solution)/shard_map/all_to_all | solution.py:226
  14.0 1.6 %load.2.table_ref = bf16[2048,512]{1,0:T(8,128)(2,1)S(1)} custom-call(bf16[2048,512]{1,0:T(8,128)(2,1)} %refs_0_.2), custom_call_target="tpu_custom_call" | custom-call | bytes 2097152 | tf_op jit(solution)/shard_map/load/pallas_call | solution.py:159
  15.7 6.3 %all-to-all-done = s32[32,1,64]{2,1,0:T(1,128)S(1)} async-done(((s32[32,1,64]{2,1,0:T(1,128)}), s32[32,1,64]{2,1,0:T(1,128)S(1)}, u32[]{:S(2)}, u32[]{:S(2)}) %all-to-all-start) | async-done | bytes 8224 | tf_op jit(solution)/shard_map/all_to_all | solution.py:226
  21.9 0.8 %rows.1 = bf16[16,2,8,256]{3,2,1,0:T(8,128)(2,1)S(1)} custom-call(s32[1]{0:T(128)} %bitcast.idx_ref, s32[32,64]{1,0:T(8,128)S(1)} %bitcast.16, bf16[2048,512]{1,0:T(8,128)(2,1)S(1)} %load.2.table_ref, s32[1,128]{1,0:T(1,128)S(1)} %live.1._.len_ref), custom_call_target="tpu_custom_call" | custom-call | tf_op jit(solution)/shard_map/rows/pallas_call | solution.py:236
  22.7 12.1 %all_to_all.16 = bf16[32,8,256]{2,1,0:T(8,128)(2,1)S(1)} all-to-all(bf16[32,8,256]{2,1,0:T(8,128)(2,1)S(1)} %bitcast.10), channel_id=1, replica_groups=mesh['dp'=32,'tensor'=8] {'dp'}, dimensions={0} | all-to-all | bytes 262144 | tf_op jit(solution)/shard_map/all_to_all | solution.py:244
  34.8 0.0 copy-done.4
  34.8 0.4 pick.1.refs_2_.refs_0_._.emb_ref
  35.2 1.3 %collective-permute-start.2 = (bf16[64,512]{1,0:T(8,128)(2,1)S(1)}, bf16[64,512]{1,0:T(8,128)(2,1)S(1)}, u32[]{:S(2)}, u32[]{:S(2)}) collective-permute-start(bf16[64,512]{1,0:T(8,128)(2,1)S(1)} %pick.1.refs_2_.refs_0_._.emb_ref), channel_id=1, source_target_pairs={{0,6},{1,3},{2,4},{3,1},{4,2},{5,7},{6,0},{7,5},{8,14},{9,11},{10,... | collective-permute-start | bytes 196616 | tf_op jit(solution)/shard_map/ppermute | solution.py:265
  36.5 2.5 %collective-permute-start.1 = (bf16[64,512]{1,0:T(8,128)(2,1)S(1)}, bf16[64,512]{1,0:T(8,128)(2,1)S(1)}, u32[]{:S(2)}, u32[]{:S(2)}) collective-permute-start(bf16[64,512]{1,0:T(8,128)(2,1)S(1)} %pick.1.refs_2_.refs_0_._.emb_ref), channel_id=1, source_target_pairs={{0,4},{1,5},{2,6},{3,7},{4,0},{5,1},{6,2},{7,3},{8,12},{9,13},{10,... | collective-permute-start | bytes 196616 | tf_op jit(solution)/shard_map/ppermute | solution.py:265
  39.0 0.2 collective-permute-start
  39.2 0.0 copy-done.5
  39.2 0.0 copy-done.3
  39.2 0.2 place.1
  39.4 3.5 %load.3 = (bf16[4096,512]{1,0:T(8,128)(2,1)S(1)}, bf16[512,4096]{1,0:T(8,128)(2,1)S(1)}) custom-call(bf16[4096,512]{1,0:T(8,128)(2,1)} %refs_0_.3, bf16[512,4096]{1,0:T(8,128)(2,1)} %refs_1_.1, bf16[64,512]{1,0:T(8,128)(2,1)S(1)} %pick.1.refs_2_.refs_0_._.emb_ref), custom_call_target="tpu_custom_call" | custom-call | bytes 8388608 | tf_op jit(solution)/shard_map/load/pallas_call | solution.py:159
  42.9 0.0 copy-start
  42.9 0.0 copy-start.1
  42.9 0.0 copy-start.2
  42.9 0.0 collective-permute-done.2.refs_3_
  42.9 0.0 collective-permute-done.1.refs_2_
  42.9 1.2 %collective-permute-done.refs_1_ = bf16[64,512]{1,0:T(8,128)(2,1)S(1)} collective-permute-done((bf16[64,512]{1,0:T(8,128)(2,1)S(1)}, bf16[64,512]{1,0:T(8,128)(2,1)S(1)}, u32[]{:S(2)}, u32[]{:S(2)}) %collective-permute-start) | collective-permute-done | bytes 65568 | tf_op jit(solution)/shard_map/ppermute | solution.py:265
  44.2 3.1 %collective-permute-start.3 = (bf16[4,64,512]{2,1,0:T(8,128)(2,1)S(1)}, bf16[4,64,512]{2,1,0:T(8,128)(2,1)S(1)}, u32[]{:S(2)}, u32[]{:S(2)}) collective-permute-start(bf16[4,64,512]{2,1,0:T(8,128)(2,1)S(1)} %stack.1.mine_ref), channel_id=1, source_target_pairs={{0,1},{1,0},{2,3},{3,2},{4,5},{5,4},{6,7},{7,6},{8,9},{9,8},{10,11... | collective-permute-start | bytes 786440 | tf_op jit(solution)/shard_map/ppermute | solution.py:266
  47.3 0.1 fusion
  47.4 0.1 pad_maximum_fusion
  47.5 0.9 %collective-permute-done.3.other_ref = bf16[4,64,512]{2,1,0:T(8,128)(2,1)S(1)} collective-permute-done((bf16[4,64,512]{2,1,0:T(8,128)(2,1)S(1)}, bf16[4,64,512]{2,1,0:T(8,128)(2,1)S(1)}, u32[]{:S(2)}, u32[]{:S(2)}) %collective-permute-start.3) | collective-permute-done | bytes 262176 | tf_op jit(solution)/shard_map/ppermute | solution.py:266
  48.4 0.0 copy-done
  48.4 0.0 copy-done.1
  48.4 0.0 copy-done.2
  48.4 2.5 %layer.1 = (bf16[64,512]{1,0:T(8,128)(2,1)S(1)}, bf16[4,64,512]{2,1,0:T(8,128)(2,1)S(1)}) custom-call(s32[1,128]{1,0:T(1,128)S(1)} %live.1._.len_ref, bf16[4,64,512]{2,1,0:T(8,128)(2,1)S(1)} %stack.1.mine_ref, bf16[4,64,512]{2,1,0:T(8,128)(2,1)S(1)} %collective-permute-done.3.other_ref, bf16[1,4096]{1,0:T(2,128)(2,1)S(1)} %reshape.22.gain_ref, ...), custom_call_target="tpu_custom_call" | custom-call | tf_op jit(solution)/shard_map/layer/pallas_call | solution.py:284
  51.0 0.5 collective-permute-start.4
  51.5 0.5 project.1.own_ref
  52.0 0.7 %collective-permute-done.4.came_ref = bf16[4,64,512]{2,1,0:T(8,128)(2,1)S(1)} collective-permute-done((bf16[4,64,512]{2,1,0:T(8,128)(2,1)S(1)}, bf16[4,64,512]{2,1,0:T(8,128)(2,1)S(1)}, u32[]{:S(2)}, u32[]{:S(2)}) %collective-permute-start.4) | collective-permute-done | bytes 262176 | tf_op jit(solution)/shard_map/ppermute | solution.py:299
  52.7 1.9 %collective-permute-start.5 = (bf16[64,512]{1,0:T(8,128)(2,1)S(1)}, bf16[64,512]{1,0:T(8,128)(2,1)S(1)}, u32[]{:S(2)}, u32[]{:S(2)}) collective-permute-start(bf16[64,512]{1,0:T(8,128)(2,1)S(1)} %get-tuple-element.22), channel_id=1, source_target_pairs={{0,2},{1,7},{2,0},{3,5},{4,6},{5,3},{6,4},{7,1},{8,10},{9,15},{10,... | collective-permute-start | bytes 196616 | tf_op jit(solution)/shard_map/ppermute | solution.py:319
  54.6 0.5 collective-permute-start.6
  55.1 0.9 %collective-permute-start.7 = (bf16[64,512]{1,0:T(8,128)(2,1)S(1)}, bf16[64,512]{1,0:T(8,128)(2,1)S(1)}, u32[]{:S(2)}, u32[]{:S(2)}) collective-permute-start(bf16[64,512]{1,0:T(8,128)(2,1)S(1)} %get-tuple-element.24), channel_id=1, source_target_pairs={{0,6},{1,3},{2,4},{3,1},{4,2},{5,7},{6,0},{7,5},{8,14},{9,11},{10,... | collective-permute-start | bytes 196616 | tf_op jit(solution)/shard_map/ppermute | solution.py:319
  56.0 1.1 %collective-permute-done.5.refs_0_ = bf16[64,512]{1,0:T(8,128)(2,1)S(1)} collective-permute-done((bf16[64,512]{1,0:T(8,128)(2,1)S(1)}, bf16[64,512]{1,0:T(8,128)(2,1)S(1)}, u32[]{:S(2)}, u32[]{:S(2)}) %collective-permute-start.5) | collective-permute-done | bytes 65568 | tf_op jit(solution)/shard_map/ppermute | solution.py:319
  57.1 2.8 %collective-permute-done.6.refs_1_ = bf16[64,512]{1,0:T(8,128)(2,1)S(1)} collective-permute-done((bf16[64,512]{1,0:T(8,128)(2,1)S(1)}, bf16[64,512]{1,0:T(8,128)(2,1)S(1)}, u32[]{:S(2)}, u32[]{:S(2)}) %collective-permute-start.6) | collective-permute-done | bytes 65568 | tf_op jit(solution)/shard_map/ppermute | solution.py:319
  59.9 0.0 collective-permute-done.7.refs_2_
  59.9 0.7 %final.1 = bf16[64,512]{1,0:T(8,128)(2,1)} custom-call(bf16[64,512]{1,0:T(8,128)(2,1)S(1)} %pick.1.refs_2_.refs_0_._.emb_ref, f32[64,512]{1,0:T(8,128)S(1)} %get-tuple-element.21.own_ref, bf16[64,512]{1,0:T(8,128)(2,1)S(1)} %collective-permute-done.5.refs_0_, bf16[64,512]{1,0:T(8,128)(2,1)S(1)} %collective-permute-done.6.refs_1_, ...), custom_call_target="tpu_custom_call" | custom-call | tf_op jit(solution)/shard_map/final/pallas_call | solution.py:320
  (5 shorter events, 0.1 us)
Async XLA Ops:
  0.0 34.8 %copy-start.4 = (s32[1,64]{1,0:T(1,128)S(1)}, s32[1,64]{1,0:T(1,128)}, u32[]{:S(2)}) copy-start(s32[1,64]{1,0:T(1,128)} %ids_ref.3) | copy-start | bytes 772
  0.0 39.2 %copy-start.5 = (bf16[4096]{0:T(1024)(128)(2,1)S(1)}, bf16[4096]{0:T(1024)(128)(2,1)}, u32[]{:S(2)}) copy-start(bf16[4096]{0:T(1024)(128)(2,1)} %param.14) | copy-start | bytes 24580
  0.0 39.2 %copy-start.3 = (s32[1,64,64]{2,1,0:T(8,128)S(1)}, s32[1,64,64]{2,1,0:T(8,128)}, u32[]{:S(2)}) copy-start(s32[1,64,64]{2,1,0:T(8,128)} %param.11) | copy-start | bytes 49156
  1.3 20.6 %all-to-all-start = ((s32[32,1,64]{2,1,0:T(1,128)}), s32[32,1,64]{2,1,0:T(1,128)S(1)}, u32[]{:S(2)}, u32[]{:S(2)}) async-start(s32[32,1,64]{2,1,0:T(1,128)} %bitcast.17), calls=%async_computation | async-start | bytes 32768 | tf_op jit(solution)/shard_map/all_to_all | solution.py:226
  35.2 7.7 %collective-permute-start.2 = (bf16[64,512]{1,0:T(8,128)(2,1)S(1)}, bf16[64,512]{1,0:T(8,128)(2,1)S(1)}, u32[]{:S(2)}, u32[]{:S(2)}) collective-permute-start(bf16[64,512]{1,0:T(8,128)(2,1)S(1)} %pick.1.refs_2_.refs_0_._.emb_ref), channel_id=1, source_target_pairs={{0,6},{1,3},{2,4},{3,1},{4,2},{5,7},{6,0},{7,5},{8,14},{9,11},{10,... | collective-permute-start | bytes 196616 | tf_op jit(solution)/shard_map/ppermute | solution.py:265
  36.5 6.4 %collective-permute-start.1 = (bf16[64,512]{1,0:T(8,128)(2,1)S(1)}, bf16[64,512]{1,0:T(8,128)(2,1)S(1)}, u32[]{:S(2)}, u32[]{:S(2)}) collective-permute-start(bf16[64,512]{1,0:T(8,128)(2,1)S(1)} %pick.1.refs_2_.refs_0_._.emb_ref), channel_id=1, source_target_pairs={{0,4},{1,5},{2,6},{3,7},{4,0},{5,1},{6,2},{7,3},{8,12},{9,13},{10,... | collective-permute-start | bytes 196616 | tf_op jit(solution)/shard_map/ppermute | solution.py:265
  39.0 5.2 %collective-permute-start = (bf16[64,512]{1,0:T(8,128)(2,1)S(1)}, bf16[64,512]{1,0:T(8,128)(2,1)S(1)}, u32[]{:S(2)}, u32[]{:S(2)}) collective-permute-start(bf16[64,512]{1,0:T(8,128)(2,1)S(1)} %pick.1.refs_2_.refs_0_._.emb_ref), channel_id=1, source_target_pairs={{0,2},{1,7},{2,0},{3,5},{4,6},{5,3},{6,4},{7,1},{8,10},{9,15},{10,... | collective-permute-start | bytes 196616 | tf_op jit(solution)/shard_map/ppermute | solution.py:265
  42.9 5.6 %copy-start = (bf16[2,4096,128]{2,1,0:T(8,128)(2,1)S(1)}, bf16[2,4096,128]{2,1,0:T(8,128)(2,1)}, u32[]{:S(2)}) copy-start(bf16[2,4096,128]{2,1,0:T(8,128)(2,1)} %wkv_ref.1) | copy-start | bytes 6291460
  42.9 5.6 %copy-start.1 = (bf16[1,1,1024,128]{3,2,1,0:T(8,128)(2,1)S(1)}, bf16[1,1,1024,128]{3,2,1,0:T(8,128)(2,1)}, u32[]{:S(2)}) copy-start(bf16[1,1,1024,128]{3,2,1,0:T(8,128)(2,1)} %param.18) | copy-start | bytes 786436
  42.9 5.5 %copy-start.2 = (bf16[1,1,1024,128]{3,2,1,0:T(8,128)(2,1)S(1)}, bf16[1,1,1024,128]{3,2,1,0:T(8,128)(2,1)}, u32[]{:S(2)}) copy-start(bf16[1,1,1024,128]{3,2,1,0:T(8,128)(2,1)} %param.19) | copy-start | bytes 786436
  44.2 4.3 %collective-permute-start.3 = (bf16[4,64,512]{2,1,0:T(8,128)(2,1)S(1)}, bf16[4,64,512]{2,1,0:T(8,128)(2,1)S(1)}, u32[]{:S(2)}, u32[]{:S(2)}) collective-permute-start(bf16[4,64,512]{2,1,0:T(8,128)(2,1)S(1)} %stack.1.mine_ref), channel_id=1, source_target_pairs={{0,1},{1,0},{2,3},{3,2},{4,5},{5,4},{6,7},{7,6},{8,9},{9,8},{10,11... | collective-permute-start | bytes 786440 | tf_op jit(solution)/shard_map/ppermute | solution.py:266
  51.0 1.6 %collective-permute-start.4 = (bf16[4,64,512]{2,1,0:T(8,128)(2,1)S(1)}, bf16[4,64,512]{2,1,0:T(8,128)(2,1)S(1)}, u32[]{:S(2)}, u32[]{:S(2)}) collective-permute-start(bf16[4,64,512]{2,1,0:T(8,128)(2,1)S(1)} %get-tuple-element.20), channel_id=1, source_target_pairs={{0,1},{1,0},{2,3},{3,2},{4,5},{5,4},{6,7},{7,6},{8,9},{9,8},{10,11... | collective-permute-start | bytes 786440 | tf_op jit(solution)/shard_map/ppermute | solution.py:299
  52.7 4.4 %collective-permute-start.5 = (bf16[64,512]{1,0:T(8,128)(2,1)S(1)}, bf16[64,512]{1,0:T(8,128)(2,1)S(1)}, u32[]{:S(2)}, u32[]{:S(2)}) collective-permute-start(bf16[64,512]{1,0:T(8,128)(2,1)S(1)} %get-tuple-element.22), channel_id=1, source_target_pairs={{0,2},{1,7},{2,0},{3,5},{4,6},{5,3},{6,4},{7,1},{8,10},{9,15},{10,... | collective-permute-start | bytes 196616 | tf_op jit(solution)/shard_map/ppermute | solution.py:319
  54.6 5.3 %collective-permute-start.6 = (bf16[64,512]{1,0:T(8,128)(2,1)S(1)}, bf16[64,512]{1,0:T(8,128)(2,1)S(1)}, u32[]{:S(2)}, u32[]{:S(2)}) collective-permute-start(bf16[64,512]{1,0:T(8,128)(2,1)S(1)} %get-tuple-element.23), channel_id=1, source_target_pairs={{0,4},{1,5},{2,6},{3,7},{4,0},{5,1},{6,2},{7,3},{8,12},{9,13},{10,... | collective-permute-start | bytes 196616 | tf_op jit(solution)/shard_map/ppermute | solution.py:319
  55.1 4.8 %collective-permute-start.7 = (bf16[64,512]{1,0:T(8,128)(2,1)S(1)}, bf16[64,512]{1,0:T(8,128)(2,1)S(1)}, u32[]{:S(2)}, u32[]{:S(2)}) collective-permute-start(bf16[64,512]{1,0:T(8,128)(2,1)S(1)} %get-tuple-element.24), channel_id=1, source_target_pairs={{0,6},{1,3},{2,4},{3,1},{4,2},{5,7},{6,0},{7,5},{8,14},{9,11},{10,... | collective-permute-start | bytes 196616 | tf_op jit(solution)/shard_map/ppermute | solution.py:319
